TPU v7x, 512 devices: a whole 4x4x16 slice. The times are simulated.
512 devices in a mesh: span: 8 (over z_hi, y), stream: 64 (over x, z_lo, core).
Axes of the slice: x: 4, y: 4, z: 16 (z_hi: 2, z_lo: 8; z = z_hi * 8 + z_lo), core: 2. Of those that a mesh axis runs over, the one named last changes fastest.
Arguments:
- velocity: float32 [3, 32, 512, 256], P(None, 'span', 'stream'), may hold values from -32 to 32
- strain: float32 [6, 32, 512, 256], P(None, 'span', 'stream'), may hold values from -4 to 4
- row_bins: int32 [512], P('stream'), may hold values from 0 to 63, never falling along the last dimension, each value on 1 to 16 neighbouring positions
- cotangent: float32 [6, 32, 512, 256], P(None, 'span', 'stream'), may hold values from -6 to 6
Outputs:
- model_residual: float32 [6, 32, 512, 256], P(None, 'span', 'stream')
- velocity_grad: float32 [3, 32, 512, 256], P(None, 'span', 'stream')
Inputs may be any that keep to these rules, and one draw needn't show every extreme that they name: `row_bins`: bins never fall along the rows, and every bin holds 1 to 16 rows.
All inputs are finite; a program needn't handle non-finite values.
Results may differ from a plain program's by a relative error of at most 0.0003.
Values sent between devices are 32-bit elements; how exact they have to be, the bound alone decides.
A program may use at most 64 MiB of HBM per device.

v0:
```python
import jax
import jax.numpy as jnp
import numpy as np
from jax import lax
from jax.sharding import PartitionSpec as P

NBINS = 64


FILTER_ALPHA = 0.45
CENTER_WEIGHT = 0.95
SIDE_WEIGHT = 0.475
STRAIN_FLOOR = 0.25
EPSILON = 1e-06
INDEX_PAIRS = ((0, 0), (0, 1), (0, 2), (1, 1), (1, 2), (2, 2))
PAIR_WEIGHTS = (1.0, 2.0, 2.0, 1.0, 2.0, 1.0)
HIGHEST = lax.Precision.HIGHEST


def extended(array, sides, width):
    for axis, dim in sides:
        peers, length = (lax.axis_size(axis), array.shape[dim])
        up = [(i, (i + 1) % peers) for i in range(peers)]
        down = [(j, i) for i, j in up]
        last = lax.slice_in_dim(array, length - width, length, axis=dim)
        first = lax.slice_in_dim(array, 0, width, axis=dim)
        before = lax.ppermute(last, axis, up)
        after = lax.ppermute(first, axis, down)
        array = jnp.concatenate([before, array, after], axis=dim)
    return array


def invert_table(matrix):
    extent = matrix.shape[0]
    augmented = np.concatenate([np.array(matrix), np.eye(extent)], axis=1)
    for column in range(extent):
        pivot_row = column + int(np.argmax(np.abs(augmented[column:, column])))
        swapped = augmented[[pivot_row, column]]
        augmented[[column, pivot_row]] = swapped
        augmented[column] = augmented[column] / augmented[column, column]
        for row_index in range(extent):
            if row_index != column:
                augmented[row_index] = (
                    augmented[row_index] - augmented[row_index, column] * augmented[column]
                )
    return augmented[:, extent:]


def loop_tables(cell_count, devices):
    local_system = np.eye(cell_count) + FILTER_ALPHA * (
        np.eye(cell_count, k=1) + np.eye(cell_count, k=-1)
    )
    local_inverse = invert_table(local_system)
    first_column = local_inverse[:, 0]
    last_column = local_inverse[:, cell_count - 1]
    unknowns = 2 * devices
    coupling = np.eye(unknowns)
    for device in range(devices):
        previous = (device - 1) % devices
        following = (device + 1) % devices
        for which_end, cell_index in ((0, 0), (1, cell_count - 1)):
            target = 2 * device + which_end
            coupling[target, 2 * previous + 1] += FILTER_ALPHA * first_column[cell_index]
            coupling[target, 2 * following] += FILTER_ALPHA * last_column[cell_index]
    reduced = invert_table(coupling)
    selectors = np.stack(
        [
            reduced[[2 * ((device - 1) % devices) + 1, 2 * ((device + 1) % devices)], :]
            for device in range(devices)
        ]
    )
    return (
        jnp.asarray(local_inverse, jnp.float32),
        jnp.asarray(first_column, jnp.float32),
        jnp.asarray(last_column, jnp.float32),
        jnp.asarray(selectors, jnp.float32),
    )


def rim_side(values):
    padded = extended(values, (("span", 1),), 1)
    return CENTER_WEIGHT * values + SIDE_WEIGHT * (padded[:, 2:] + padded[:, :-2])


def solve_loop(values, tables, own_index):
    local_inverse, first_column, last_column, selectors = tables
    particular = jnp.einsum("ij,fjyx->fiyx", local_inverse, values, precision=HIGHEST)
    end_values = jnp.stack([particular[:, 0], particular[:, -1]], axis=0)
    selector = lax.dynamic_index_in_dim(selectors, own_index, 0, keepdims=False)
    gathered_piece = lax.all_gather(end_values, "span", axis=0, tiled=True)
    columns = lax.slice_in_dim(selector, 0, gathered_piece.shape[0], axis=1)
    neighbours = jnp.zeros_like(end_values) + jnp.einsum(
        "ae,efyx->afyx", columns, gathered_piece, precision=HIGHEST
    )
    previous = neighbours[0]
    following = neighbours[1]
    solved = particular - FILTER_ALPHA * (
        first_column[None, :, None, None] * previous[:, None]
        + last_column[None, :, None, None] * following[:, None]
    )
    return (solved, previous, following)


def solve_back(values, tables, own_index):
    local_inverse, first_column, last_column, selectors = tables
    selector = lax.dynamic_index_in_dim(selectors, own_index, 0, keepdims=False)
    near_bar = -FILTER_ALPHA * jnp.stack(
        [
            jnp.einsum("i,fiyx->fyx", first_column, values, precision=HIGHEST),
            jnp.einsum("i,fiyx->fyx", last_column, values, precision=HIGHEST),
        ],
        axis=0,
    )
    columns = lax.slice_in_dim(selector, 0, 2 * lax.axis_size("span"), axis=1)
    end_bar = lax.psum_scatter(
        jnp.einsum("ae,afyx->efyx", columns, near_bar, precision=HIGHEST),
        "span",
        scatter_dimension=0,
        tiled=True,
    )
    particular_bar = values.at[:, 0].add(end_bar[0]).at[:, -1].add(end_bar[1])
    return jnp.einsum("ji,fjyx->fiyx", local_inverse, particular_bar, precision=HIGHEST)


def smooth(values, tables, own_index):
    return solve_loop(rim_side(values), tables, own_index)[0]


def unsmooth(values, tables, own_index):
    return rim_side(solve_back(values, tables, own_index))


def on_device(velocity, strain, row_bins, cotangent):
    tables = loop_tables(velocity.shape[1], lax.axis_size("span"))
    own_index = lax.axis_index("span")
    weights = jnp.asarray(PAIR_WEIGHTS, jnp.float32)[:, None, None, None]
    products = jnp.stack([velocity[former] * velocity[latter] for former, latter in INDEX_PAIRS])
    size_field = jnp.sqrt(
        jnp.maximum(2.0 * jnp.sum(weights * strain * strain, axis=0), STRAIN_FLOOR)
    )
    fields = jnp.concatenate([velocity, products, size_field[None]], axis=0)
    filtered = smooth(fields, tables, own_index)
    coarse = jnp.stack([filtered[former] * filtered[latter] for former, latter in INDEX_PAIRS])
    leonard = filtered[3:9] - coarse
    model_term = products - coarse + 2.0 * (4.0 * filtered[9] - size_field)[None] * strain
    onehot = (row_bins[:, None] == jnp.arange(NBINS, dtype=jnp.int32)[None, :]).astype(jnp.float32)
    cross_local = jnp.dot(
        jnp.sum(weights * leonard * model_term, axis=(0, 1, 3)), onehot, precision=HIGHEST
    )
    square_local = jnp.dot(
        jnp.sum(weights * model_term * model_term, axis=(0, 1, 3)), onehot, precision=HIGHEST
    )
    blame_local = jnp.dot(
        jnp.sum(cotangent * model_term, axis=(0, 1, 3)), onehot, precision=HIGHEST
    )
    cross_bins, square_bins, blame_bins = lax.psum(
        (cross_local, square_local, blame_local), ("span", "stream")
    )
    denominator = square_bins + EPSILON
    coefficient = cross_bins / denominator
    row_coefficient = jnp.dot(onehot, coefficient, precision=HIGHEST)[None, None, :, None]
    residual = leonard - row_coefficient * model_term
    coefficient_bar = -blame_bins
    cross_bar = coefficient_bar / denominator
    square_bar = -coefficient_bar * coefficient / denominator
    row_cross = jnp.dot(onehot, cross_bar, precision=HIGHEST)[None, None, :, None]
    row_square = jnp.dot(onehot, square_bar, precision=HIGHEST)[None, None, :, None]
    leonard_bar = cotangent + row_cross * weights * model_term
    model_bar = (
        -row_coefficient * cotangent
        + row_cross * weights * leonard
        + 2.0 * row_square * weights * model_term
    )
    zero_field = jnp.zeros_like(velocity[0])
    coarse_bar = [zero_field, zero_field, zero_field]
    for position, (former, latter) in enumerate(INDEX_PAIRS):
        combined = leonard_bar[position] + model_bar[position]
        coarse_bar[former] = coarse_bar[former] - combined * filtered[latter]
        coarse_bar[latter] = coarse_bar[latter] - combined * filtered[former]
    pulled = unsmooth(
        jnp.concatenate([jnp.stack(coarse_bar), leonard_bar], axis=0), tables, own_index
    )
    gradient_parts = [pulled[0], pulled[1], pulled[2]]
    for position, (former, latter) in enumerate(INDEX_PAIRS):
        through = pulled[3 + position] + model_bar[position]
        gradient_parts[former] = gradient_parts[former] + through * velocity[latter]
        gradient_parts[latter] = gradient_parts[latter] + through * velocity[former]
    return (residual, jnp.stack(gradient_parts))


def solution(mesh):
    return jax.shard_map(
        on_device,
        mesh=mesh,
        in_specs=(
            P(None, "span", "stream", None),
            P(None, "span", "stream", None),
            P("stream"),
            P(None, "span", "stream", None),
        ),
        out_specs=(P(None, "span", "stream", None), P(None, "span", "stream", None)),
        check_vma=False,
    )
```

profile of v0, /device:TPU:130, one launch (start us, length us, event | category | flops | bytes accessed | tf_op | source)
XLA Modules:
  0.0 400.0 jit_solution(6443093883510731724)
XLA Ops:
  7.2 0.8 fusion.61
  8.0 0.9 constant_dynamic-update-slice_fusion.7
  8.9 1.1 fusion.10
  10.4 13.4 %collective-permute-start = (f32[10,1,8,256]{3,2,1,0:T(8,128)S(1)}, f32[10,1,8,256]{3,2,1,0:T(8,128)S(1)}, u32[]{:S(2)}, u32[]{:S(2)}) collective-permute-start(f32[10,1,8,256]{3,2,1,0:T(8,128)S(1)} %get-tuple-element.54), channel_id=1, source_target_pairs={{64,0},{128,64},{192,128},{256,192},{320,256},{384,320},{448,384},... | collective-permute-start | bytes 245768 | tf_op jit(solution)/shard_map/ppermute | solution.py:28
  23.7 1.9 collective-permute-start.1
  25.7 0.1 collective-permute-done
  25.8 16.1 %collective-permute-done.1 = f32[10,1,8,256]{3,2,1,0:T(8,128)S(1)} collective-permute-done((f32[10,1,8,256]{3,2,1,0:T(8,128)S(1)}, f32[10,1,8,256]{3,2,1,0:T(8,128)S(1)}, u32[]{:S(2)}, u32[]{:S(2)}) %collective-permute-start.1) | collective-permute-done | bytes 81952 | tf_op jit(solution)/shard_map/ppermute | solution.py:27
  42.0 0.7 convolution_bitcast_fusion
  42.7 0.1 slice_bitcast_fusion.1
  42.9 0.2 pad_maximum_fusion.5
  43.0 0.7 copy.44
  43.8 84.5 %all-gather.2.cloned.1.call-done = f32[16,10,8,256]{3,2,1,0:T(8,128)} async-done(((f32[2,10,8,256]{3,2,1,0:T(8,128)}), f32[16,10,8,256]{3,2,1,0:T(8,128)}) %all-gather.2.cloned.1.call-update) | async-done | bytes 1310736 | tf_op jit(solution)/shard_map/all_gather | solution.py:90
  128.3 2.7 fusion
  131.1 0.1 fusion.59
  131.2 0.2 multiply_subtract_fusion
  131.6 0.3 copy-done
  132.0 0.1 copy-done.1
  132.1 0.4 fusion.11
  132.5 0.2 convolution_bitcast_fusion.6
  132.6 0.2 convolution_bitcast_fusion.7
  132.8 0.2 convolution_bitcast_fusion.4
  133.0 107.1 %all-reduce = (f32[64]{0:T(128)S(1)}, f32[64]{0:T(128)S(1)}, f32[64]{0:T(128)S(1)}) all-reduce(f32[64]{0:T(128)S(1)} %convolution_bitcast_fusion.7, f32[64]{0:T(128)S(1)} %convolution_bitcast_fusion.6, f32[64]{0:T(128)S(1)} %convolution_bitcast_fusion.4), channel_id=1, replica_groups=mesh['span'=8,'stream'=64] {'span','stream'}, use_global_device_ids=true, to_apply=%region_2.3 | all-reduce | flops 192 | bytes 1536 | tf_op jit(solution)/shard_map/psum | solution.py:156
  240.1 0.2 convolution_bitcast_fusion.3
  240.3 0.2 fusion.2
  240.5 0.2 fusion.62
  240.7 0.1 broadcast_multiply_fusion
  240.7 0.2 multiply_add_fusion
  241.1 0.1 pad_maximum_fusion.4
  241.2 0.2 copy-done.5
  241.4 0.6 fusion.64
  242.1 0.6 fusion.63
  242.8 1.9 fusion.12
  244.8 1.7 copy.50
  246.5 108.7 %reduce-scatter.2.cloned.1.call-done = f32[2,9,8,256]{3,2,1,0:T(8,128)} async-done(((f32[16,9,8,256]{3,2,1,0:T(8,128)}), f32[2,9,8,256]{3,2,1,0:T(8,128)}) %reduce-scatter.2.cloned.1.call-update) | async-done | bytes 147472 | tf_op jit(solution)/shard_map/reduce_scatter | solution.py:115
  355.2 0.9 fusion.60
  356.1 0.1 slice_add_fusion.1
  356.3 2.2 scatter-add.6
  358.4 0.1 slice_add_fusion
  358.6 2.2 scatter-add.9
  360.7 0.7 convolution_bitcast_fusion.1
  361.4 0.1 fusion.58
  361.5 12.4 %collective-permute-start.2 = (f32[9,1,8,256]{3,1,2,0:T(1,128)S(1)}, f32[9,1,8,256]{3,1,2,0:T(1,128)S(1)}, u32[]{:S(2)}, u32[]{:S(2)}) collective-permute-start(f32[9,1,8,256]{3,1,2,0:T(1,128)S(1)} %get-tuple-element.56), channel_id=1, source_target_pairs={{64,0},{128,64},{192,128},{256,192},{320,256},{384,320},{448,384},... | collective-permute-start | bytes 221192 | tf_op jit(solution)/shard_map/ppermute | solution.py:28
  373.9 1.9 collective-permute-start.3
  375.9 0.7 copy.54
  376.6 15.4 %collective-permute-done.3 = f32[9,1,8,256]{3,1,2,0:T(1,128)S(1)} collective-permute-done((f32[9,1,8,256]{3,1,2,0:T(1,128)S(1)}, f32[9,1,8,256]{3,1,2,0:T(1,128)S(1)}, u32[]{:S(2)}, u32[]{:S(2)}) %collective-permute-start.3) | collective-permute-done | bytes 73760 | tf_op jit(solution)/shard_map/ppermute | solution.py:27
  392.0 0.3 fusion.9
  392.4 0.1 fusion.20
  392.5 0.7 copy.55
  (52 shorter events, 1.0 us)
Async XLA Ops:
  7.2 121.1 %all-gather.2.cloned.1.call-start = ((), (), s32[]{:S(2)}) async-start(), calls=%async_computation.1 | async-start | bytes 1474560 | tf_op jit(solution)/shard_map/all_gather | solution.py:90
  8.9 33.1 %copy-start.2 = (f32[4,4,1,1]{1,0,3,2:T(4,128)S(1)}, f32[4,4,1,1]{1,0,3,2:T(4,128)}, u32[]{:S(2)}) copy-start(f32[4,4,1,1]{1,0,3,2:T(4,128)} %constant.110) | copy-start | bytes 196
  10.4 15.4 %collective-permute-start = (f32[10,1,8,256]{3,2,1,0:T(8,128)S(1)}, f32[10,1,8,256]{3,2,1,0:T(8,128)S(1)}, u32[]{:S(2)}, u32[]{:S(2)}) collective-permute-start(f32[10,1,8,256]{3,2,1,0:T(8,128)S(1)} %get-tuple-element.54), channel_id=1, source_target_pairs={{64,0},{128,64},{192,128},{256,192},{320,256},{384,320},{448,384},... | collective-permute-start | bytes 245768 | tf_op jit(solution)/shard_map/ppermute | solution.py:28
  23.7 18.2 %collective-permute-start.1 = (f32[10,1,8,256]{3,2,1,0:T(8,128)S(1)}, f32[10,1,8,256]{3,2,1,0:T(8,128)S(1)}, u32[]{:S(2)}, u32[]{:S(2)}) collective-permute-start(f32[10,1,8,256]{3,2,1,0:T(8,128)S(1)} %get-tuple-element.55), channel_id=1, source_target_pairs={{0,64},{64,128},{128,192},{192,256},{256,320},{320,384},{384,448},... | collective-permute-start | bytes 245768 | tf_op jit(solution)/shard_map/ppermute | solution.py:27
  43.0 88.2 %copy-start.6 = (f32[4]{0:T(128)S(1)}, f32[4]{0:T(128)}, u32[]{:S(2)}) copy-start(f32[4]{0:T(128)} %constant.103.clone) | copy-start | bytes 52
  43.0 88.2 %copy-start.7 = (f32[4]{0:T(128)S(1)}, f32[4]{0:T(128)}, u32[]{:S(2)}) copy-start(f32[4]{0:T(128)} %constant.102.clone) | copy-start | bytes 52
  43.7 311.5 %reduce-scatter.2.cloned.1.call-start = ((), (), s32[]{:S(2)}) async-start(), calls=%async_computation.2 | async-start | bytes 1327104 | tf_op jit(solution)/shard_map/reduce_scatter | solution.py:115
  131.0 0.9 copy-start
  131.0 1.0 copy-start.1
  131.0 1.0 copy-start.3
  131.2 1.2 copy-start.8
  240.7 0.7 copy-start.5
  241.0 1.1 copy-start.4
  361.5 15.1 %collective-permute-start.2 = (f32[9,1,8,256]{3,1,2,0:T(1,128)S(1)}, f32[9,1,8,256]{3,1,2,0:T(1,128)S(1)}, u32[]{:S(2)}, u32[]{:S(2)}) collective-permute-start(f32[9,1,8,256]{3,1,2,0:T(1,128)S(1)} %get-tuple-element.56), channel_id=1, source_target_pairs={{64,0},{128,64},{192,128},{256,192},{320,256},{384,320},{448,384},... | collective-permute-start | bytes 221192 | tf_op jit(solution)/shard_map/ppermute | solution.py:28
  373.9 18.0 %collective-permute-start.3 = (f32[9,1,8,256]{3,1,2,0:T(1,128)S(1)}, f32[9,1,8,256]{3,1,2,0:T(1,128)S(1)}, u32[]{:S(2)}, u32[]{:S(2)}) collective-permute-start(f32[9,1,8,256]{3,1,2,0:T(1,128)S(1)} %get-tuple-element.57), channel_id=1, source_target_pairs={{0,64},{64,128},{128,192},{192,256},{256,320},{320,384},{384,448},... | collective-permute-start | bytes 221192 | tf_op jit(solution)/shard_map/ppermute | solution.py:27
Sparse Core Ops, SparseCore 0:
  43.9 84.3 all-gather.1
  246.6 108.5 reduce-scatter.1
where the time goes:
time: 400 us
  waiting for transfers between devices  225 us (56%)
  blocking collectives  107 us (27%)
  starting transfers between devices  29.7 us (7%)
  between operations  14.5 us (4%)
  local copies, waits for them, and re-layouts  12 us (3%)
  matrix products  8.42 us (2%)
    reduce_scatter x1, waiting for transfers between devices, solve_back(): lax.psum_scatter(jnp.einsum('ae,afyx->efyx', columns, near_bar, precision...  109 us
    psum x1, blocking collectives, on_device(): lax.psum((cross_local, square_local, blame_local), ('span', 'stream'))  107 us
    all_gather x1, waiting for transfers between devices, solve_loop(): gathered_piece = lax.all_gather(end_values, 'span', axis=0, tiled=True)  84.5 us
    ppermute x2, waiting for transfers between devices, extended(): before = lax.ppermute(last, axis, up)  31.5 us
    ppermute x2, starting transfers between devices, extended(): after = lax.ppermute(first, axis, down)  25.8 us
  transfers between devices with their start and end apart: 6, of which 6 were waited for; matrix products, arithmetic and copies ran while one was open for 0% of the time, Pallas kernels for 0%

commit v1 on v0

v1 whole, which is shorter than its diff:
```python
import jax
import jax.numpy as jnp
from jax import lax
from jax.experimental import pallas as pl
from jax.experimental.pallas import tpu as pltpu
from jax.sharding import PartitionSpec as P

ALPHA = 0.45
CENTER_WEIGHT = 0.95
SIDE_WEIGHT = 0.475
STRAIN_FLOOR = 0.25
EPSILON = 1e-06
PAIRS = ((0, 0), (0, 1), (0, 2), (1, 1), (1, 2), (2, 2))
WEIGHTS = (1.0, 2.0, 2.0, 1.0, 2.0, 1.0)
MESH = pl.DeviceIdType.MESH

ROOT = ((1.0 - 4.0 * ALPHA * ALPHA) ** 0.5 - 1.0) / (2.0 * ALPHA)
GREEN = 1.0 / (1.0 - 4.0 * ALPHA * ALPHA) ** 0.5
SCALE = SIDE_WEIGHT / ALPHA
REST = SCALE - CENTER_WEIGHT
OWN = SCALE + REST * GREEN
SWEEP = -REST * GREEN
CELLS, RING, GROUPS = 4, 4, 2
STEP = ROOT ** CELLS
AROUND = STEP ** RING
CLOSE = 1.0 / (1.0 - AROUND**GROUPS)
STREAM_STEPS = (-2, -1, 1, 2)


def ends(cells):
    right, left = cells[0], cells[3]
    for i in (1, 2, 3):
        right = cells[i] + ROOT * right
        left = cells[3 - i] + ROOT * left
    return right, left


def filtered_cells(cells, before, after):
    up, down = [], []
    for i in range(CELLS):
        before = cells[i] + ROOT * before
        after = cells[CELLS - 1 - i] + ROOT * after
        up.append(before)
        down.append(after)
    return [OWN * cells[i] + SWEEP * (up[i] + down[CELLS - 1 - i]) for i in range(CELLS)]


def carry(blocks):
    total = blocks[0]
    for p in (1, 2, 3):
        total = blocks[p] + STEP * total
    return total


def kernel(vel, strain, bins, cot, res, grad,
           fields, filt, leo, mod, back,
           e1, rb1, pa1, zb1, g1, ag1,
           ec, rbc, pac, zbc,
           e2, rb2, pa2, zb2, g2, ag2,
           t1, ty, t2, ts, t3, tz,
           send, recv):
    span, stream = lax.axis_index("span"), lax.axis_index("stream")
    h, y = span // RING, lax.rem(span, RING)
    mirror = lax.rem(y, 2)
    place = y + mirror * (RING - 1 - 2 * y)

    def ring_peer(delta):
        return lax.rem(y + delta, RING)

    def ring_id(other):
        return (h * RING + other, stream)

    across = ((GROUPS - 1 - h) * RING + y, stream)

    def stream_id(step):
        turn = (lax.rem(stream, 16) + step + 16) // 16 - 1
        flip = turn * turn
        return ((h + flip - 2 * h * flip) * RING + y, lax.rem(stream + step + 64, 64))

    copies = []

    def push(src, dst, device):
        n = len(copies)
        copy = pltpu.make_async_remote_copy(
            src_ref=src, dst_ref=dst, send_sem=send.at[n], recv_sem=recv.at[n],
            device_id=device, device_id_type=MESH)
        copy.start()
        copies.append(copy)
        return copy

    def scatter(src, dst):
        out = []
        for delta in (2, 1, 3):
            other = ring_peer(delta)
            slot = y + lax.rem(other, 2) * (RING - 1 - 2 * y)
            out.append(push(src.at[other], dst.at[slot], ring_id(other)))
        dst[place] = src[y]
        return out

    def spread(src, dst):
        out = []
        for delta in (2, 1, 3):
            other = ring_peer(delta)
            slot = other + mirror * (RING - 1 - 2 * other)
            out.append(push(src.at[slot], dst.at[y], ring_id(other)))
        dst[y] = src[place]
        return out

    def arrive(group):
        for copy in group:
            copy.wait_recv()

    def keep_ends(buf, at, cells):
        right, left = ends(cells)
        for half in (0, 1):
            lanes = slice(128 * half, 128 * half + 128)
            buf[2 * half, at] = right[..., lanes]
            buf[2 * half + 1, at] = left[..., lanes]

    barrier = pltpu.get_barrier_semaphore()
    greeted = [ring_id(ring_peer(d)) for d in (1, 2, 3)] + [across] + [stream_id(s) for s in STREAM_STEPS]
    for device in greeted:
        pl.semaphore_signal(barrier, inc=1, device_id=device, device_id_type=MESH)

    for a in range(3):
        fields[a] = vel[a]
    total = jnp.zeros((CELLS, 8, 256), jnp.float32)
    for k, (a, b) in enumerate(PAIRS):
        fields[3 + k] = vel[a] * vel[b]
        total = total + WEIGHTS[k] * (strain[k] * strain[k])
    fields[9] = jnp.sqrt(jnp.maximum(2.0 * total, STRAIN_FLOOR))
    for f in range(10):
        keep_ends(e1, f, [fields[f, i] for i in range(CELLS)])
    for k in range(6):
        keep_ends(ec, k, [cot[k, i] for i in range(CELLS)])
    row = lax.broadcasted_iota(jnp.int32, (8, 128), 0)
    lane = lax.broadcasted_iota(jnp.int32, (8, 128), 1)
    own_bins = jnp.zeros((8, 128), jnp.float32)
    for i in range(8):
        own_bins = jnp.where(row == i, bins[i].astype(jnp.float32), own_bins)

    pl.semaphore_wait(barrier, len(greeted))

    first = scatter(e1, rb1)
    first_cot = scatter(ec, rbc)
    arrive(first)
    pa1[...] = carry([rb1[p] for p in range(RING)])
    over = push(pa1, zb1, across)
    arrive(first_cot)
    pac[...] = carry([rbc[p] for p in range(RING)])
    over_cot = push(pac, zbc, across)
    arrive([over])
    entering = CLOSE * (zb1[...] + AROUND * pa1[...])
    g1[0] = entering
    for p in range(RING - 1):
        entering = rb1[p] + STEP * entering
        g1[p + 1] = entering
    arrive(spread(g1, ag1))

    for f in (9, 0, 1, 2):
        for half in (0, 1):
            lanes = slice(128 * half, 128 * half + 128)
            out = filtered_cells([fields[f, i, :, lanes] for i in range(CELLS)],
                                 ag1[2 * half, f], ag1[2 * half + 1, f])
            for i in range(CELLS):
                filt[f % 9 if f < 9 else 3, i, :, lanes] = out[i]
    cross = jnp.zeros((8, 256), jnp.float32)
    square = jnp.zeros((8, 256), jnp.float32)
    blame = jnp.zeros((8, 256), jnp.float32)
    for k, (a, b) in enumerate(PAIRS):
        f = 3 + k
        halves = []
        for half in (0, 1):
            lanes = slice(128 * half, 128 * half + 128)
            halves.append(filtered_cells([fields[f, i, :, lanes] for i in range(CELLS)],
                                         ag1[2 * half, f], ag1[2 * half + 1, f]))
        for i in range(CELLS):
            coarse = filt[a, i] * filt[b, i]
            leonard = jnp.concatenate([halves[0][i], halves[1][i]], axis=-1) - coarse
            size = fields[9, i]
            model = fields[f, i] - coarse + 2.0 * (4.0 * filt[3, i] - size) * strain[k, i]
            leo[k, i] = leonard
            mod[k, i] = model
            cross = cross + WEIGHTS[k] * (leonard * model)
            square = square + WEIGHTS[k] * (model * model)
            blame = blame + cot[k, i] * model

    def over_lanes(values):
        return jnp.sum(values[:, :128] + values[:, 128:], axis=-1, keepdims=True)

    t1[...] = jnp.where(lane == 0, over_lanes(cross),
                        jnp.where(lane == 1, over_lanes(square),
                                  jnp.where(lane == 2, over_lanes(blame), own_bins)))
    rows_out = [push(t1, ty.at[d - 1], ring_id(ring_peer(d))) for d in (2, 1, 3)]

    for k in range(6):
        keep_ends(e2, k, [WEIGHTS[k] * mod[k, i] for i in range(CELLS)])
    for a in range(3):
        with_cot, with_sum, with_model = [], [], []
        for i in range(CELLS):
            u = v = w = None
            for k, (former, latter) in enumerate(PAIRS):
                if a not in (former, latter):
                    continue
                other = latter if former == a else former
                factor = filt[other, i] * (2.0 if former == latter else 1.0)
                weighted = WEIGHTS[k] * factor
                terms = (cot[k, i] * factor, (mod[k, i] + leo[k, i]) * weighted, mod[k, i] * weighted)
                u, v, w = terms if u is None else (u + terms[0], v + terms[1], w + terms[2])
            with_cot.append(u)
            with_sum.append(v)
            with_model.append(w)
            back[0, a, i] = u
            back[1, a, i] = v
            back[2, a, i] = w
        keep_ends(e2, 6 + a, with_cot)
        keep_ends(e2, 9 + a, with_sum)
        keep_ends(e2, 12 + a, with_model)
    second = scatter(e2, rb2)

    arrive(rows_out)
    t2[...] = jnp.where(lane == 3, own_bins, t1[...] + ty[0] + ty[1] + ty[2])
    near = [push(t2, ts.at[n], stream_id(s)) for n, s in enumerate(STREAM_STEPS)]
    arrive(second)
    pa2[...] = carry([rb2[p] for p in range(RING)])
    over2 = push(pa2, zb2, across)
    arrive(near)
    sums = jnp.zeros((8, 128), jnp.float32)
    for n in range(5):
        tile = t2[...] if n == 4 else ts[n]
        tile_bins = jnp.broadcast_to(tile[:, 3:4], (8, 128))
        for j in range(8):
            sums = sums + jnp.where(own_bins == tile_bins[j:j + 1], tile[j:j + 1], 0.0)
    t3[...] = sums
    over3 = push(t3, tz, across)
    arrive([over3])
    sums = sums + tz[...]
    denominator = jnp.broadcast_to(sums[:, 1:2], (8, 128)) + EPSILON
    coefficient = jnp.broadcast_to(sums[:, 0:1], (8, 128)) / denominator
    row_cross = -jnp.broadcast_to(sums[:, 2:3], (8, 128)) / denominator
    row_square = -2.0 * row_cross * coefficient
    spare = coefficient - 1.0

    def combined(part, part_cot):
        coarse = spare * part(6, 9) - row_cross * part(9, 12) - row_square * part(12, 15)
        return coarse, part_cot() + row_cross * part(0, 6)

    arrive([over_cot, over2])
    blocks = [combined(lambda m, n, p=p: rb2[p, m:n], lambda p=p: rbc[p]) for p in range(RING)]
    others = combined(lambda m, n: zb2[m:n], lambda: zbc[...])
    for part, at in ((0, slice(0, 3)), (1, slice(3, 9))):
        entering = CLOSE * (others[part] + AROUND * carry([block[part] for block in blocks]))
        g2[0, at] = entering
        for p in range(RING - 1):
            entering = blocks[p][part] + STEP * entering
            g2[p + 1, at] = entering
    last = spread(g2, ag2)

    def wide(values):
        return jnp.concatenate([values, values], axis=-1)

    coefficient, row_cross, row_square, spare = (
        wide(coefficient), wide(row_cross), wide(row_square), wide(spare))
    for a in range(3):
        for i in range(CELLS):
            back[0, a, i] = spare * back[0, a, i] - row_cross * back[1, a, i] - row_square * back[2, a, i]
    for k in range(6):
        for i in range(CELLS):
            leonard, model, bar = leo[k, i], mod[k, i], cot[k, i]
            res[k, i] = leonard - coefficient * model
            weighted = WEIGHTS[k] * row_cross
            leo[k, i] = bar + weighted * model
            mod[k, i] = weighted * leonard - coefficient * bar + (WEIGHTS[k] * row_square) * model
    arrive(last)
    for half in (0, 1):
        lanes = slice(128 * half, 128 * half + 128)
        sums = []
        for a in range(3):
            sums.append(filtered_cells([back[0, a, i, :, lanes] for i in range(CELLS)],
                                       ag2[2 * half, a], ag2[2 * half + 1, a]))
        for k, (a, b) in enumerate(PAIRS):
            pulled = filtered_cells([leo[k, i, :, lanes] for i in range(CELLS)],
                                    ag2[2 * half, 3 + k], ag2[2 * half + 1, 3 + k])
            for i in range(CELLS):
                through = pulled[i] + mod[k, i, :, lanes]
                sums[a][i] = sums[a][i] + through * vel[b, i, :, lanes]
                sums[b][i] = sums[b][i] + through * vel[a, i, :, lanes]
        for a in range(3):
            for i in range(CELLS):
                grad[a, i, :, lanes] = sums[a][i]
    for copy in copies:
        copy.wait_send()


def on_device(velocity, strain, row_bins, cotangent):
    def buf(*shape):
        return pltpu.VMEM(shape, jnp.float32)

    vmem = pl.BlockSpec(memory_space=pltpu.VMEM)
    scratch = [
        buf(10, 4, 8, 256), buf(4, 4, 8, 256), buf(6, 4, 8, 256), buf(6, 4, 8, 256), buf(3, 3, 4, 8, 256),
        buf(4, 10, 8, 128), buf(4, 10, 8, 128), buf(10, 8, 128), buf(10, 8, 128), buf(4, 10, 8, 128),
        buf(4, 10, 8, 128),
        buf(4, 6, 8, 128), buf(4, 6, 8, 128), buf(6, 8, 128), buf(6, 8, 128),
        buf(4, 15, 8, 128), buf(4, 15, 8, 128), buf(15, 8, 128), buf(15, 8, 128), buf(4, 9, 8, 128),
        buf(4, 9, 8, 128),
        buf(8, 128), buf(3, 8, 128), buf(8, 128), buf(4, 8, 128), buf(8, 128), buf(8, 128),
        pltpu.SemaphoreType.DMA((32,)), pltpu.SemaphoreType.DMA((32,)),
    ]
    return pl.pallas_call(
        kernel,
        out_shape=(
            jax.ShapeDtypeStruct(strain.shape, jnp.float32),
            jax.ShapeDtypeStruct(velocity.shape, jnp.float32),
        ),
        in_specs=[vmem, vmem, pl.BlockSpec(memory_space=pltpu.SMEM), vmem],
        out_specs=(vmem, vmem),
        scratch_shapes=scratch,
        compiler_params=pltpu.CompilerParams(
            collective_id=1, has_side_effects=True, vmem_limit_bytes=32 * 1024 * 1024),
        cost_estimate=pl.CostEstimate(flops=3_000_000, bytes_accessed=800_000, transcendentals=8192),
    )(velocity, strain, row_bins, cotangent)


def solution(mesh):
    field = P(None, "span", "stream", None)
    return jax.shard_map(
        on_device, mesh=mesh, in_specs=(field, field, P("stream"), field), out_specs=(field, field),
        check_vma=False)
```

time: 400 us -> 57.6 us (0.14)
  the two profiles are of different devices: /device:TPU:130 before, /device:TPU:32 now
where the time goes in v1:
time: 57.6 us; the launch traced here: 57.4 us
  Pallas kernels  52 us (90%)
  local copies, waits for them, and re-layouts  4.71 us (8%)
  between operations  0.65 us (1%)
    pallas_call x1, Pallas kernels, on_device(): pl.pallas_call(kernel, out_shape=(jax.ShapeDtypeStruct(strain.shape, jnp....  52 us
    unnamed x10, local copies, waits for them, and re-layouts  4.71 us

profile of v1, /device:TPU:32, one launch (start us, length us, event | category | flops | bytes accessed | tf_op | source)
XLA Modules:
  0.0 57.4 jit_solution(997706773046807162)
XLA Ops:
  0.6 0.0 copy-start
  0.6 0.9 %copy-done = f32[6,4,8,256]{3,2,1,0:T(8,128)S(1)} copy-done((f32[6,4,8,256]{3,2,1,0:T(8,128)S(1)}, f32[6,4,8,256]{3,2,1,0:T(8,128)}, u32[]{:S(2)}) %copy-start) | copy-done | bytes 196632
  1.6 0.0 copy-start.1
  1.6 0.9 %copy-done.1 = f32[6,4,8,256]{3,2,1,0:T(8,128)S(1)} copy-done((f32[6,4,8,256]{3,2,1,0:T(8,128)S(1)}, f32[6,4,8,256]{3,2,1,0:T(8,128)}, u32[]{:S(2)}) %copy-start.1) | copy-done | bytes 196632
  2.5 0.0 copy-start.2
  2.5 0.9 %copy-done.2 = f32[3,4,8,256]{3,2,1,0:T(8,128)S(1)} copy-done((f32[3,4,8,256]{3,2,1,0:T(8,128)S(1)}, f32[3,4,8,256]{3,2,1,0:T(8,128)}, u32[]{:S(2)}) %copy-start.2) | copy-done | bytes 98328
  3.4 0.0 copy-start.3
  3.4 0.7 %copy-done.3 = s32[8]{0:T(128)S(1)} copy-done((s32[8]{0:T(128)S(1)}, s32[8]{0:T(128)}, u32[]{:S(2)}) %copy-start.3) | copy-done | bytes 56
  4.0 52.0 %shard_map.59 = (f32[6,4,8,256]{3,2,1,0:T(8,128)S(1)}, f32[3,4,8,256]{3,2,1,0:T(8,128)S(1)}) custom-call(f32[3,4,8,256]{3,2,1,0:T(8,128)S(1)} %copy-done.2, f32[6,4,8,256]{3,2,1,0:T(8,128)S(1)} %copy-done, s32[8]{0:T(128)S(1)} %copy-done.3, f32[6,4,8,256]{3,2,1,0:T(8,128)S(1)} %copy-done.1), custom_call_target="tpu_custom_call" | custom-call | flops 3000000 | bytes 800000 | tf_op jit(solution)/shard_map/pallas_call | solution.py:310
  56.1 0.7 %copy.8 = f32[6,4,8,256]{3,2,1,0:T(8,128)} copy(f32[6,4,8,256]{3,2,1,0:T(8,128)S(1)} %get-tuple-element.4) | data formatting | bytes 393216
  56.8 0.6 %copy.9 = f32[3,4,8,256]{3,2,1,0:T(8,128)} copy(f32[3,4,8,256]{3,2,1,0:T(8,128)S(1)} %get-tuple-element.5) | data formatting | bytes 196608
Async XLA Ops:
  0.6 0.9 %copy-start = (f32[6,4,8,256]{3,2,1,0:T(8,128)S(1)}, f32[6,4,8,256]{3,2,1,0:T(8,128)}, u32[]{:S(2)}) copy-start(f32[6,4,8,256]{3,2,1,0:T(8,128)} %strain.1) | copy-start | bytes 589828
  1.6 0.9 %copy-start.1 = (f32[6,4,8,256]{3,2,1,0:T(8,128)S(1)}, f32[6,4,8,256]{3,2,1,0:T(8,128)}, u32[]{:S(2)}) copy-start(f32[6,4,8,256]{3,2,1,0:T(8,128)} %cot.1) | copy-start | bytes 589828
  2.5 0.9 %copy-start.2 = (f32[3,4,8,256]{3,2,1,0:T(8,128)S(1)}, f32[3,4,8,256]{3,2,1,0:T(8,128)}, u32[]{:S(2)}) copy-start(f32[3,4,8,256]{3,2,1,0:T(8,128)} %vel.1) | copy-start | bytes 294916
  3.4 0.7 %copy-start.3 = (s32[8]{0:T(128)S(1)}, s32[8]{0:T(128)}, u32[]{:S(2)}) copy-start(s32[8]{0:T(128)} %bins.1) | copy-start | bytes 100

commit v2 on v1

--- a/solution.py
+++ b/solution.py
@@ -52,13 +52,13 @@
     return total
 
 
-def kernel(vel, strain, bins, cot, res, grad,
-           fields, filt, leo, mod, back,
+def kernel(vel_in, strain_in, bins_in, cot_in, res, grad,
+           vel, strain, bins, cot, fields, filt, leo, mod, back,
            e1, rb1, pa1, zb1, g1, ag1,
            ec, rbc, pac, zbc,
            e2, rb2, pa2, zb2, g2, ag2,
            t1, ty, t2, ts, t3, tz,
-           send, recv):
+           send, recv, load, gate):
     span, stream = lax.axis_index("span"), lax.axis_index("stream")
     h, y = span // RING, lax.rem(span, RING)
     mirror = lax.rem(y, 2)
@@ -117,10 +117,33 @@
             buf[2 * half, at] = right[..., lanes]
             buf[2 * half + 1, at] = left[..., lanes]
 
+    core = lax.rem(stream, 2)
+    this_chip = stream - core
+
+    def greet(sem, device):
+        pl.semaphore_signal(sem, inc=1, device_id=device, device_id_type=MESH)
+
+    def chip_id(step):
+        there, position = stream_id(2 * step)
+        return (there, position - core)
+
     barrier = pltpu.get_barrier_semaphore()
-    greeted = [ring_id(ring_peer(d)) for d in (1, 2, 3)] + [across] + [stream_id(s) for s in STREAM_STEPS]
-    for device in greeted:
-        pl.semaphore_signal(barrier, inc=1, device_id=device, device_id_type=MESH)
+    greet(barrier, (across[0], this_chip))
+    for d in (2, 1, 3):
+        greet(barrier, (h * RING + ring_peer(d), this_chip + 1))
+    greet(barrier, chip_id(-1))
+    greet(barrier, chip_id(1))
+
+    @pl.when(core == 0)
+    def _():
+        greet(barrier, (span, stream + 1))
+
+    loads = [pltpu.make_async_copy(src, dst, load.at[n]) for n, (src, dst) in enumerate(
+        ((vel_in, vel), (strain_in, strain), (cot_in, cot), (bins_in, bins)))]
+    for one in loads:
+        one.start()
+    for one in loads:
+        one.wait()
 
     for a in range(3):
         fields[a] = vel[a]
@@ -139,12 +162,29 @@
     for i in range(8):
         own_bins = jnp.where(row == i, bins[i].astype(jnp.float32), own_bins)
 
-    pl.semaphore_wait(barrier, len(greeted))
+    @pl.when(core == 1)
+    def _():
+        pl.semaphore_wait(barrier, 2 * (RING - 1) + 1)
+        greet(gate, (span, stream - 1))
+
+    @pl.when(core == 0)
+    def _():
+        pl.semaphore_wait(gate, 1)
 
     first = scatter(e1, rb1)
     first_cot = scatter(ec, rbc)
     arrive(first)
     pa1[...] = carry([rb1[p] for p in range(RING)])
+
+    @pl.when(core == 0)
+    def _():
+        pl.semaphore_wait(barrier, 2 + 2 * 2)
+        greet(gate, (span, stream + 1))
+
+    @pl.when(core == 1)
+    def _():
+        pl.semaphore_wait(gate, 1)
+
     over = push(pa1, zb1, across)
     arrive(first_cot)
     pac[...] = carry([rbc[p] for p in range(RING)])
@@ -297,7 +337,9 @@
         return pltpu.VMEM(shape, jnp.float32)
 
     vmem = pl.BlockSpec(memory_space=pltpu.VMEM)
+    hbm = pl.BlockSpec(memory_space=pltpu.HBM)
     scratch = [
+        buf(3, 4, 8, 256), buf(6, 4, 8, 256), pltpu.SMEM((8,), jnp.int32), buf(6, 4, 8, 256),
         buf(10, 4, 8, 256), buf(4, 4, 8, 256), buf(6, 4, 8, 256), buf(6, 4, 8, 256), buf(3, 3, 4, 8, 256),
         buf(4, 10, 8, 128), buf(4, 10, 8, 128), buf(10, 8, 128), buf(10, 8, 128), buf(4, 10, 8, 128),
         buf(4, 10, 8, 128),
@@ -305,21 +347,22 @@
         buf(4, 15, 8, 128), buf(4, 15, 8, 128), buf(15, 8, 128), buf(15, 8, 128), buf(4, 9, 8, 128),
         buf(4, 9, 8, 128),
         buf(8, 128), buf(3, 8, 128), buf(8, 128), buf(4, 8, 128), buf(8, 128), buf(8, 128),
-        pltpu.SemaphoreType.DMA((32,)), pltpu.SemaphoreType.DMA((32,)),
+        pltpu.SemaphoreType.DMA((32,)), pltpu.SemaphoreType.DMA((32,)), pltpu.SemaphoreType.DMA((4,)),
+        pltpu.SemaphoreType.REGULAR,
     ]
     return pl.pallas_call(
         kernel,
         out_shape=(
-            jax.ShapeDtypeStruct(strain.shape, jnp.float32),
-            jax.ShapeDtypeStruct(velocity.shape, jnp.float32),
+            pltpu.VMEM(strain.shape, jnp.float32),
+            pltpu.VMEM(velocity.shape, jnp.float32),
         ),
-        in_specs=[vmem, vmem, pl.BlockSpec(memory_space=pltpu.SMEM), vmem],
+        in_specs=[hbm, hbm, hbm, hbm],
         out_specs=(vmem, vmem),
         scratch_shapes=scratch,
         compiler_params=pltpu.CompilerParams(
             collective_id=1, has_side_effects=True, vmem_limit_bytes=32 * 1024 * 1024),
         cost_estimate=pl.CostEstimate(flops=3_000_000, bytes_accessed=800_000, transcendentals=8192),
-    )(velocity, strain, row_bins, cotangent)
+    )(*[pltpu.with_memory_space_constraint(v, pltpu.HBM) for v in (velocity, strain, row_bins, cotangent)])
 
 
 def solution(mesh):

time: 57.6 us -> 54.1 us (0.939)
  the two profiles are of different devices: /device:TPU:32 before, /device:TPU:8 now
where the time goes in v2:
time: 54.1 us; the launch traced here: 54 us
  Pallas kernels  52 us (96%)
  local copies, waits for them, and re-layouts  1.32 us (2%)
  between operations  0.64 us (1%)
    pallas_call x1, Pallas kernels, on_device(): pl.pallas_call(kernel, out_shape=(pltpu.VMEM(strain.shape, jnp.float32),...  52 us
    unnamed x2, local copies, waits for them, and re-layouts  1.32 us

profile of v2, /device:TPU:8, one launch (start us, length us, event | category | flops | bytes accessed | tf_op | source)
XLA Modules:
  0.0 54.0 jit_solution(12088697422919501828)
XLA Ops:
  0.6 52.0 %shard_map.59 = (f32[6,4,8,256]{3,2,1,0:T(8,128)S(1)}, f32[3,4,8,256]{3,2,1,0:T(8,128)S(1)}) custom-call(f32[3,4,8,256]{3,2,1,0:T(8,128)} %vel_in.1, f32[6,4,8,256]{3,2,1,0:T(8,128)} %strain_in.1, s32[8]{0:T(128)} %bins_in.1, f32[6,4,8,256]{3,2,1,0:T(8,128)} %cot_in.1), custom_call_target="tpu_custom_call" | custom-call | flops 3000000 | bytes 800000 | tf_op jit(solution)/shard_map/pallas_call | solution.py:353
  52.6 0.7 %copy.8 = f32[6,4,8,256]{3,2,1,0:T(8,128)} copy(f32[6,4,8,256]{3,2,1,0:T(8,128)S(1)} %get-tuple-element.2) | data formatting | bytes 393216
  53.3 0.6 %copy.9 = f32[3,4,8,256]{3,2,1,0:T(8,128)} copy(f32[3,4,8,256]{3,2,1,0:T(8,128)S(1)} %get-tuple-element.3) | data formatting | bytes 196608

commit v3 on v2

--- a/solution.py
+++ b/solution.py
@@ -57,7 +57,7 @@
            e1, rb1, pa1, zb1, g1, ag1,
            ec, rbc, pac, zbc,
            e2, rb2, pa2, zb2, g2, ag2,
-           t1, ty, t2, ts, t3, tz,
+           t1, ts, t3, tz,
            send, recv, load, gate):
     span, stream = lax.axis_index("span"), lax.axis_index("stream")
     h, y = span // RING, lax.rem(span, RING)
@@ -88,22 +88,22 @@
         copies.append(copy)
         return copy
 
-    def scatter(src, dst):
+    def scatter(src, dst, at):
         out = []
         for delta in (2, 1, 3):
             other = ring_peer(delta)
             slot = y + lax.rem(other, 2) * (RING - 1 - 2 * y)
-            out.append(push(src.at[other], dst.at[slot], ring_id(other)))
-        dst[place] = src[y]
+            out.append(push(src.at[other, at], dst.at[slot, at], ring_id(other)))
+        dst[place, at] = src[y, at]
         return out
 
-    def spread(src, dst):
+    def spread(src, dst, at):
         out = []
         for delta in (2, 1, 3):
             other = ring_peer(delta)
             slot = other + mirror * (RING - 1 - 2 * other)
-            out.append(push(src.at[slot], dst.at[y], ring_id(other)))
-        dst[y] = src[place]
+            out.append(push(src.at[slot, at], dst.at[y, at], ring_id(other)))
+        dst[y, at] = src[place, at]
         return out
 
     def arrive(group):
@@ -149,13 +149,11 @@
         fields[a] = vel[a]
     total = jnp.zeros((CELLS, 8, 256), jnp.float32)
     for k, (a, b) in enumerate(PAIRS):
-        fields[3 + k] = vel[a] * vel[b]
+        fields[4 + k] = vel[a] * vel[b]
         total = total + WEIGHTS[k] * (strain[k] * strain[k])
-    fields[9] = jnp.sqrt(jnp.maximum(2.0 * total, STRAIN_FLOOR))
+    fields[3] = jnp.sqrt(jnp.maximum(2.0 * total, STRAIN_FLOOR))
     for f in range(10):
         keep_ends(e1, f, [fields[f, i] for i in range(CELLS)])
-    for k in range(6):
-        keep_ends(ec, k, [cot[k, i] for i in range(CELLS)])
     row = lax.broadcasted_iota(jnp.int32, (8, 128), 0)
     lane = lax.broadcasted_iota(jnp.int32, (8, 128), 1)
     own_bins = jnp.zeros((8, 128), jnp.float32)
@@ -171,44 +169,49 @@
     def _():
         pl.semaphore_wait(gate, 1)
 
-    first = scatter(e1, rb1)
-    first_cot = scatter(ec, rbc)
-    arrive(first)
-    pa1[...] = carry([rb1[p] for p in range(RING)])
-
-    @pl.when(core == 0)
-    def _():
-        pl.semaphore_wait(barrier, 2 + 2 * 2)
-        greet(gate, (span, stream + 1))
-
-    @pl.when(core == 1)
-    def _():
-        pl.semaphore_wait(gate, 1)
-
-    over = push(pa1, zb1, across)
-    arrive(first_cot)
-    pac[...] = carry([rbc[p] for p in range(RING)])
-    over_cot = push(pac, zbc, across)
-    arrive([over])
-    entering = CLOSE * (zb1[...] + AROUND * pa1[...])
-    g1[0] = entering
-    for p in range(RING - 1):
-        entering = rb1[p] + STEP * entering
-        g1[p + 1] = entering
-    arrive(spread(g1, ag1))
-
-    for f in (9, 0, 1, 2):
+    early, late = slice(0, 4), slice(4, 10)
+    scattered = [scatter(e1, rb1, at) for at in (early, late)]
+    for k in range(6):
+        keep_ends(ec, k, [cot[k, i] for i in range(CELLS)])
+    crossed, arrived = [], []
+    for at, group in zip((early, late), scattered):
+        arrive(group)
+        pa1[at] = carry([rb1[p, at] for p in range(RING)])
+        if not crossed:
+            @pl.when(core == 0)
+            def _():
+                pl.semaphore_wait(barrier, 2 + 2 * 2)
+                greet(gate, (span, stream + 1))
+
+            @pl.when(core == 1)
+            def _():
+                pl.semaphore_wait(gate, 1)
+
+        crossed.append(push(pa1.at[at], zb1.at[at], across))
+    for at, copy in zip((early, late), crossed):
+        arrive([copy])
+        entering = CLOSE * (zb1[at] + AROUND * pa1[at])
+        g1[0, at] = entering
+        for p in range(RING - 1):
+            entering = rb1[p, at] + STEP * entering
+            g1[p + 1, at] = entering
+        arrived.append(spread(g1, ag1, at))
+    first_cot = scatter(ec, rbc, slice(0, 6))
+    arrive(arrived[0])
+
+    for f in (0, 1, 2, 3):
         for half in (0, 1):
             lanes = slice(128 * half, 128 * half + 128)
             out = filtered_cells([fields[f, i, :, lanes] for i in range(CELLS)],
                                  ag1[2 * half, f], ag1[2 * half + 1, f])
             for i in range(CELLS):
-                filt[f % 9 if f < 9 else 3, i, :, lanes] = out[i]
+                filt[f, i, :, lanes] = out[i]
+    arrive(arrived[1])
     cross = jnp.zeros((8, 256), jnp.float32)
     square = jnp.zeros((8, 256), jnp.float32)
     blame = jnp.zeros((8, 256), jnp.float32)
     for k, (a, b) in enumerate(PAIRS):
-        f = 3 + k
+        f = 4 + k
         halves = []
         for half in (0, 1):
             lanes = slice(128 * half, 128 * half + 128)
@@ -217,7 +220,7 @@
         for i in range(CELLS):
             coarse = filt[a, i] * filt[b, i]
             leonard = jnp.concatenate([halves[0][i], halves[1][i]], axis=-1) - coarse
-            size = fields[9, i]
+            size = fields[3, i]
             model = fields[f, i] - coarse + 2.0 * (4.0 * filt[3, i] - size) * strain[k, i]
             leo[k, i] = leonard
             mod[k, i] = model
@@ -225,16 +228,22 @@
             square = square + WEIGHTS[k] * (model * model)
             blame = blame + cot[k, i] * model
 
+    for k in range(6):
+        keep_ends(e2, k, [WEIGHTS[k] * mod[k, i] for i in range(CELLS)])
+    early, late = slice(0, 6), slice(6, 15)
+    second = [scatter(e2, rb2, early)]
+
     def over_lanes(values):
         return jnp.sum(values[:, :128] + values[:, 128:], axis=-1, keepdims=True)
 
     t1[...] = jnp.where(lane == 0, over_lanes(cross),
                         jnp.where(lane == 1, over_lanes(square),
                                   jnp.where(lane == 2, over_lanes(blame), own_bins)))
-    rows_out = [push(t1, ty.at[d - 1], ring_id(ring_peer(d))) for d in (2, 1, 3)]
-
-    for k in range(6):
-        keep_ends(e2, k, [WEIGHTS[k] * mod[k, i] for i in range(CELLS)])
+    near = [push(t1, ts.at[n], stream_id(s)) for n, s in enumerate(STREAM_STEPS)]
+    arrive(first_cot)
+    pac[...] = carry([rbc[p] for p in range(RING)])
+    over_cot = push(pac, zbc, across)
+
     for a in range(3):
         with_cot, with_sum, with_model = [], [], []
         for i in range(CELLS):
@@ -256,45 +265,49 @@
         keep_ends(e2, 6 + a, with_cot)
         keep_ends(e2, 9 + a, with_sum)
         keep_ends(e2, 12 + a, with_model)
-    second = scatter(e2, rb2)
-
-    arrive(rows_out)
-    t2[...] = jnp.where(lane == 3, own_bins, t1[...] + ty[0] + ty[1] + ty[2])
-    near = [push(t2, ts.at[n], stream_id(s)) for n, s in enumerate(STREAM_STEPS)]
-    arrive(second)
-    pa2[...] = carry([rb2[p] for p in range(RING)])
-    over2 = push(pa2, zb2, across)
+    second.append(scatter(e2, rb2, late))
+
+    arrive(second[0])
+    pa2[early] = carry([rb2[p, early] for p in range(RING)])
+    over2 = [push(pa2.at[early], zb2.at[early], across)]
     arrive(near)
     sums = jnp.zeros((8, 128), jnp.float32)
     for n in range(5):
-        tile = t2[...] if n == 4 else ts[n]
+        tile = t1[...] if n == 4 else ts[n]
         tile_bins = jnp.broadcast_to(tile[:, 3:4], (8, 128))
         for j in range(8):
             sums = sums + jnp.where(own_bins == tile_bins[j:j + 1], tile[j:j + 1], 0.0)
     t3[...] = sums
-    over3 = push(t3, tz, across)
-    arrive([over3])
-    sums = sums + tz[...]
+    everywhere = [push(t3, tz.at[d - 1], (lax.rem(span + d, 8), stream)) for d in (4, 3, 5, 2, 6, 1, 7)]
+    arrive(second[1])
+    pa2[late] = carry([rb2[p, late] for p in range(RING)])
+    over2.append(push(pa2.at[late], zb2.at[late], across))
+    arrive(everywhere)
+    for d in range(7):
+        sums = sums + tz[d]
     denominator = jnp.broadcast_to(sums[:, 1:2], (8, 128)) + EPSILON
     coefficient = jnp.broadcast_to(sums[:, 0:1], (8, 128)) / denominator
     row_cross = -jnp.broadcast_to(sums[:, 2:3], (8, 128)) / denominator
     row_square = -2.0 * row_cross * coefficient
     spare = coefficient - 1.0
 
-    def combined(part, part_cot):
-        coarse = spare * part(6, 9) - row_cross * part(9, 12) - row_square * part(12, 15)
-        return coarse, part_cot() + row_cross * part(0, 6)
-
-    arrive([over_cot, over2])
-    blocks = [combined(lambda m, n, p=p: rb2[p, m:n], lambda p=p: rbc[p]) for p in range(RING)]
-    others = combined(lambda m, n: zb2[m:n], lambda: zbc[...])
-    for part, at in ((0, slice(0, 3)), (1, slice(3, 9))):
-        entering = CLOSE * (others[part] + AROUND * carry([block[part] for block in blocks]))
+    def adjoint(at, blocks, other):
+        entering = CLOSE * (other + AROUND * carry(blocks))
         g2[0, at] = entering
         for p in range(RING - 1):
-            entering = blocks[p][part] + STEP * entering
+            entering = blocks[p] + STEP * entering
             g2[p + 1, at] = entering
-    last = spread(g2, ag2)
+        return spread(g2, ag2, at)
+
+    def coarse_part(buf, *p):
+        return (spare * buf[(*p, slice(6, 9))] - row_cross * buf[(*p, slice(9, 12))]
+                - row_square * buf[(*p, slice(12, 15))])
+
+    arrive([over_cot, over2[0]])
+    last = adjoint(slice(3, 9), [rbc[p] + row_cross * rb2[p, 0:6] for p in range(RING)],
+                   zbc[...] + row_cross * zb2[0:6])
+    arrive([over2[1]])
+    last = last + adjoint(slice(0, 3), [coarse_part(rb2, p) for p in range(RING)], coarse_part(zb2))
 
     def wide(values):
         return jnp.concatenate([values, values], axis=-1)
@@ -346,8 +359,8 @@
         buf(4, 6, 8, 128), buf(4, 6, 8, 128), buf(6, 8, 128), buf(6, 8, 128),
         buf(4, 15, 8, 128), buf(4, 15, 8, 128), buf(15, 8, 128), buf(15, 8, 128), buf(4, 9, 8, 128),
         buf(4, 9, 8, 128),
-        buf(8, 128), buf(3, 8, 128), buf(8, 128), buf(4, 8, 128), buf(8, 128), buf(8, 128),
-        pltpu.SemaphoreType.DMA((32,)), pltpu.SemaphoreType.DMA((32,)), pltpu.SemaphoreType.DMA((4,)),
+        buf(8, 128), buf(4, 8, 128), buf(8, 128), buf(7, 8, 128),
+        pltpu.SemaphoreType.DMA((64,)), pltpu.SemaphoreType.DMA((64,)), pltpu.SemaphoreType.DMA((4,)),
         pltpu.SemaphoreType.REGULAR,
     ]
     return pl.pallas_call(

time: 54.1 us -> 50.7 us (0.937)
  the two profiles are of different devices: /device:TPU:8 before, /device:TPU:4 now
where the time goes in v3:
time: 50.7 us; the launch traced here: 50.5 us
  Pallas kernels  48.6 us (96%)
  local copies, waits for them, and re-layouts  1.32 us (3%)
  between operations  0.64 us (1%)
    pallas_call x1, Pallas kernels, on_device(): pl.pallas_call(kernel, out_shape=(pltpu.VMEM(strain.shape, jnp.float32),...  48.6 us
    unnamed x2, local copies, waits for them, and re-layouts  1.32 us

profile of v3, /device:TPU:4, one launch (start us, length us, event | category | flops | bytes accessed | tf_op | source)
XLA Modules:
  0.0 50.5 jit_solution(16053617412150928050)
XLA Ops:
  0.6 48.6 %shard_map.59 = (f32[6,4,8,256]{3,2,1,0:T(8,128)S(1)}, f32[3,4,8,256]{3,2,1,0:T(8,128)S(1)}) custom-call(f32[3,4,8,256]{3,2,1,0:T(8,128)} %vel_in.1, f32[6,4,8,256]{3,2,1,0:T(8,128)} %strain_in.1, s32[8]{0:T(128)} %bins_in.1, f32[6,4,8,256]{3,2,1,0:T(8,128)} %cot_in.1), custom_call_target="tpu_custom_call" | custom-call | flops 3000000 | bytes 800000 | tf_op jit(solution)/shard_map/pallas_call | solution.py:366
  49.2 0.7 %copy.8 = f32[6,4,8,256]{3,2,1,0:T(8,128)} copy(f32[6,4,8,256]{3,2,1,0:T(8,128)S(1)} %get-tuple-element.2) | data formatting | bytes 393216
  49.9 0.6 %copy.9 = f32[3,4,8,256]{3,2,1,0:T(8,128)} copy(f32[3,4,8,256]{3,2,1,0:T(8,128)S(1)} %get-tuple-element.3) | data formatting | bytes 196608

commit v4 on v3

--- a/solution.py
+++ b/solution.py
@@ -156,9 +156,21 @@
         keep_ends(e1, f, [fields[f, i] for i in range(CELLS)])
     row = lax.broadcasted_iota(jnp.int32, (8, 128), 0)
     lane = lax.broadcasted_iota(jnp.int32, (8, 128), 1)
+    column = lax.rem(lane, 8)
+    kind = lane // 8
     own_bins = jnp.zeros((8, 128), jnp.float32)
+    lane_bins = jnp.zeros((8, 128), jnp.float32)
     for i in range(8):
-        own_bins = jnp.where(row == i, bins[i].astype(jnp.float32), own_bins)
+        value = bins[i].astype(jnp.float32)
+        own_bins = jnp.where(row == i, value, own_bins)
+        lane_bins = jnp.where(column == i, value, lane_bins)
+
+    def packed(three):
+        wide = jnp.where(kind == 0, three[0], jnp.where(kind == 1, three[1], jnp.where(kind == 2, three[2], 0.0)))
+        return jnp.sum(jnp.where(column == row, wide, 0.0), axis=0, keepdims=True)
+
+    def columns_of(wide, mask):
+        return [jnp.sum(jnp.where(mask & (kind == q), wide, 0.0), axis=-1, keepdims=True) for q in range(3)]
 
     @pl.when(core == 1)
     def _():
@@ -171,8 +183,6 @@
 
     early, late = slice(0, 4), slice(4, 10)
     scattered = [scatter(e1, rb1, at) for at in (early, late)]
-    for k in range(6):
-        keep_ends(ec, k, [cot[k, i] for i in range(CELLS)])
     crossed, arrived = [], []
     for at, group in zip((early, late), scattered):
         arrive(group)
@@ -188,6 +198,9 @@
                 pl.semaphore_wait(gate, 1)
 
         crossed.append(push(pa1.at[at], zb1.at[at], across))
+    for k in range(6):
+        keep_ends(ec, k, [cot[k, i] for i in range(CELLS)])
+    first_cot = scatter(ec, rbc, slice(0, 6))
     for at, copy in zip((early, late), crossed):
         arrive([copy])
         entering = CLOSE * (zb1[at] + AROUND * pa1[at])
@@ -196,99 +209,101 @@
             entering = rb1[p, at] + STEP * entering
             g1[p + 1, at] = entering
         arrived.append(spread(g1, ag1, at))
-    first_cot = scatter(ec, rbc, slice(0, 6))
     arrive(arrived[0])
-
-    for f in (0, 1, 2, 3):
+    for f in range(4):
         for half in (0, 1):
             lanes = slice(128 * half, 128 * half + 128)
             out = filtered_cells([fields[f, i, :, lanes] for i in range(CELLS)],
                                  ag1[2 * half, f], ag1[2 * half + 1, f])
             for i in range(CELLS):
                 filt[f, i, :, lanes] = out[i]
-    arrive(arrived[1])
-    cross = jnp.zeros((8, 256), jnp.float32)
     square = jnp.zeros((8, 256), jnp.float32)
     blame = jnp.zeros((8, 256), jnp.float32)
     for k, (a, b) in enumerate(PAIRS):
-        f = 4 + k
+        weighted = []
+        for i in range(CELLS):
+            coarse = filt[a, i] * filt[b, i]
+            model = fields[4 + k, i] - coarse + 2.0 * (4.0 * filt[3, i] - fields[3, i]) * strain[k, i]
+            mod[k, i] = model
+            weighted.append(WEIGHTS[k] * model)
+            square = square + weighted[i] * model
+            blame = blame + cot[k, i] * model
+        keep_ends(e2, k, weighted)
+    parts = (slice(0, 6), slice(6, 12), slice(12, 15))
+    second = [scatter(e2, rb2, parts[0])]
+
+    def with_filtered(a, slot, field):
+        cells = []
+        for i in range(CELLS):
+            total = None
+            for k, (former, latter) in enumerate(PAIRS):
+                if a in (former, latter):
+                    other = latter if former == a else former
+                    term = field(k, i) * ((2.0 if former == latter else 1.0) * filt[other, i])
+                    total = term if total is None else total + term
+            back[slot, a, i] = total
+            cells.append(total)
+        keep_ends(e2, 6 + 3 * slot + a, cells)
+
+    for a in range(3):
+        with_filtered(a, 0, lambda k, i: cot[k, i])
+        with_filtered(a, 1, lambda k, i: WEIGHTS[k] * mod[k, i])
+    second.append(scatter(e2, rb2, parts[1]))
+
+    arrive(first_cot)
+    pac[...] = carry([rbc[p] for p in range(RING)])
+    over_cot = push(pac, zbc, across)
+
+    arrive(arrived[1])
+    cross = jnp.zeros((8, 256), jnp.float32)
+    for k, (a, b) in enumerate(PAIRS):
         halves = []
         for half in (0, 1):
             lanes = slice(128 * half, 128 * half + 128)
-            halves.append(filtered_cells([fields[f, i, :, lanes] for i in range(CELLS)],
-                                         ag1[2 * half, f], ag1[2 * half + 1, f]))
+            halves.append(filtered_cells([fields[4 + k, i, :, lanes] for i in range(CELLS)],
+                                         ag1[2 * half, 4 + k], ag1[2 * half + 1, 4 + k]))
         for i in range(CELLS):
-            coarse = filt[a, i] * filt[b, i]
-            leonard = jnp.concatenate([halves[0][i], halves[1][i]], axis=-1) - coarse
-            size = fields[3, i]
-            model = fields[f, i] - coarse + 2.0 * (4.0 * filt[3, i] - size) * strain[k, i]
+            leonard = jnp.concatenate([halves[0][i], halves[1][i]], axis=-1) - filt[a, i] * filt[b, i]
             leo[k, i] = leonard
-            mod[k, i] = model
-            cross = cross + WEIGHTS[k] * (leonard * model)
-            square = square + WEIGHTS[k] * (model * model)
-            blame = blame + cot[k, i] * model
-
-    for k in range(6):
-        keep_ends(e2, k, [WEIGHTS[k] * mod[k, i] for i in range(CELLS)])
-    early, late = slice(0, 6), slice(6, 15)
-    second = [scatter(e2, rb2, early)]
+            cross = cross + WEIGHTS[k] * (leonard * mod[k, i])
 
     def over_lanes(values):
         return jnp.sum(values[:, :128] + values[:, 128:], axis=-1, keepdims=True)
 
-    t1[...] = jnp.where(lane == 0, over_lanes(cross),
-                        jnp.where(lane == 1, over_lanes(square),
-                                  jnp.where(lane == 2, over_lanes(blame), own_bins)))
+    t1[0:1] = packed([over_lanes(cross), over_lanes(square), over_lanes(blame)])
+    t1[1:2] = lane_bins[0:1]
     near = [push(t1, ts.at[n], stream_id(s)) for n, s in enumerate(STREAM_STEPS)]
-    arrive(first_cot)
-    pac[...] = carry([rbc[p] for p in range(RING)])
-    over_cot = push(pac, zbc, across)
-
     for a in range(3):
-        with_cot, with_sum, with_model = [], [], []
-        for i in range(CELLS):
-            u = v = w = None
-            for k, (former, latter) in enumerate(PAIRS):
-                if a not in (former, latter):
-                    continue
-                other = latter if former == a else former
-                factor = filt[other, i] * (2.0 if former == latter else 1.0)
-                weighted = WEIGHTS[k] * factor
-                terms = (cot[k, i] * factor, (mod[k, i] + leo[k, i]) * weighted, mod[k, i] * weighted)
-                u, v, w = terms if u is None else (u + terms[0], v + terms[1], w + terms[2])
-            with_cot.append(u)
-            with_sum.append(v)
-            with_model.append(w)
-            back[0, a, i] = u
-            back[1, a, i] = v
-            back[2, a, i] = w
-        keep_ends(e2, 6 + a, with_cot)
-        keep_ends(e2, 9 + a, with_sum)
-        keep_ends(e2, 12 + a, with_model)
-    second.append(scatter(e2, rb2, late))
-
-    arrive(second[0])
-    pa2[early] = carry([rb2[p, early] for p in range(RING)])
-    over2 = [push(pa2.at[early], zb2.at[early], across)]
+        with_filtered(a, 2, lambda k, i: WEIGHTS[k] * leo[k, i])
+    second.append(scatter(e2, rb2, parts[2]))
+
+    over2 = []
+
+    def cross_part(n):
+        at = parts[n]
+        arrive(second[n])
+        pa2[at] = carry([rb2[p, at] for p in range(RING)])
+        over2.append(push(pa2.at[at], zb2.at[at], across))
+
+    cross_part(0)
     arrive(near)
-    sums = jnp.zeros((8, 128), jnp.float32)
-    for n in range(5):
-        tile = t1[...] if n == 4 else ts[n]
-        tile_bins = jnp.broadcast_to(tile[:, 3:4], (8, 128))
-        for j in range(8):
-            sums = sums + jnp.where(own_bins == tile_bins[j:j + 1], tile[j:j + 1], 0.0)
-    t3[...] = sums
+    wide = jnp.where(own_bins == t1[1:2], t1[0:1], 0.0)
+    for n in range(4):
+        wide = wide + jnp.where(own_bins == ts[n, 1:2], ts[n, 0:1], 0.0)
+    t3[...] = packed(columns_of(wide, True))
     everywhere = [push(t3, tz.at[d - 1], (lax.rem(span + d, 8), stream)) for d in (4, 3, 5, 2, 6, 1, 7)]
-    arrive(second[1])
-    pa2[late] = carry([rb2[p, late] for p in range(RING)])
-    over2.append(push(pa2.at[late], zb2.at[late], across))
+    cross_part(1)
+    cross_part(2)
     arrive(everywhere)
+    total = t3[...]
     for d in range(7):
-        sums = sums + tz[d]
-    denominator = jnp.broadcast_to(sums[:, 1:2], (8, 128)) + EPSILON
-    coefficient = jnp.broadcast_to(sums[:, 0:1], (8, 128)) / denominator
-    row_cross = -jnp.broadcast_to(sums[:, 2:3], (8, 128)) / denominator
+        total = total + tz[d]
+    sums = columns_of(jnp.broadcast_to(total, (8, 128)), column == row)
+    denominator = jnp.broadcast_to(sums[1], (8, 128)) + EPSILON
+    coefficient = jnp.broadcast_to(sums[0], (8, 128)) / denominator
+    row_cross = -jnp.broadcast_to(sums[2], (8, 128)) / denominator
     row_square = -2.0 * row_cross * coefficient
+    row_model = row_cross + row_square
     spare = coefficient - 1.0
 
     def adjoint(at, blocks, other):
@@ -300,23 +315,23 @@
         return spread(g2, ag2, at)
 
     def coarse_part(buf, *p):
-        return (spare * buf[(*p, slice(6, 9))] - row_cross * buf[(*p, slice(9, 12))]
-                - row_square * buf[(*p, slice(12, 15))])
+        return (spare * buf[(*p, slice(6, 9))] - row_model * buf[(*p, slice(9, 12))]
+                - row_cross * buf[(*p, slice(12, 15))])
 
     arrive([over_cot, over2[0]])
     last = adjoint(slice(3, 9), [rbc[p] + row_cross * rb2[p, 0:6] for p in range(RING)],
                    zbc[...] + row_cross * zb2[0:6])
-    arrive([over2[1]])
+    arrive(over2[1:])
     last = last + adjoint(slice(0, 3), [coarse_part(rb2, p) for p in range(RING)], coarse_part(zb2))
 
     def wide(values):
         return jnp.concatenate([values, values], axis=-1)
 
-    coefficient, row_cross, row_square, spare = (
-        wide(coefficient), wide(row_cross), wide(row_square), wide(spare))
+    coefficient, row_cross, row_square, row_model, spare = (
+        wide(coefficient), wide(row_cross), wide(row_square), wide(row_model), wide(spare))
     for a in range(3):
         for i in range(CELLS):
-            back[0, a, i] = spare * back[0, a, i] - row_cross * back[1, a, i] - row_square * back[2, a, i]
+            back[0, a, i] = spare * back[0, a, i] - row_model * back[1, a, i] - row_cross * back[2, a, i]
     for k in range(6):
         for i in range(CELLS):
             leonard, model, bar = leo[k, i], mod[k, i], cot[k, i]
@@ -359,7 +374,7 @@
         buf(4, 6, 8, 128), buf(4, 6, 8, 128), buf(6, 8, 128), buf(6, 8, 128),
         buf(4, 15, 8, 128), buf(4, 15, 8, 128), buf(15, 8, 128), buf(15, 8, 128), buf(4, 9, 8, 128),
         buf(4, 9, 8, 128),
-        buf(8, 128), buf(4, 8, 128), buf(8, 128), buf(7, 8, 128),
+        buf(2, 128), buf(4, 2, 128), buf(1, 128), buf(7, 1, 128),
         pltpu.SemaphoreType.DMA((64,)), pltpu.SemaphoreType.DMA((64,)), pltpu.SemaphoreType.DMA((4,)),
         pltpu.SemaphoreType.REGULAR,
     ]

time: 50.7 us -> 48 us (0.947)
  the two profiles are of different devices: /device:TPU:4 before, /device:TPU:8 now
where the time goes in v4:
time: 48 us; the launch traced here: 47.9 us
  Pallas kernels  45.9 us (96%)
  local copies, waits for them, and re-layouts  1.32 us (3%)
  between operations  0.64 us (1%)
    pallas_call x1, Pallas kernels, on_device(): pl.pallas_call(kernel, out_shape=(pltpu.VMEM(strain.shape, jnp.float32),...  45.9 us
    unnamed x2, local copies, waits for them, and re-layouts  1.32 us

profile of v4, /device:TPU:8, one launch (start us, length us, event | category | flops | bytes accessed | tf_op | source)
XLA Modules:
  0.0 47.9 jit_solution(11730087050663118931)
XLA Ops:
  0.6 45.9 %shard_map.59 = (f32[6,4,8,256]{3,2,1,0:T(8,128)S(1)}, f32[3,4,8,256]{3,2,1,0:T(8,128)S(1)}) custom-call(f32[3,4,8,256]{3,2,1,0:T(8,128)} %vel_in.1, f32[6,4,8,256]{3,2,1,0:T(8,128)} %strain_in.1, s32[8]{0:T(128)} %bins_in.1, f32[6,4,8,256]{3,2,1,0:T(8,128)} %cot_in.1), custom_call_target="tpu_custom_call" | custom-call | flops 3000000 | bytes 800000 | tf_op jit(solution)/shard_map/pallas_call | solution.py:381
  46.6 0.7 %copy.8 = f32[6,4,8,256]{3,2,1,0:T(8,128)} copy(f32[6,4,8,256]{3,2,1,0:T(8,128)S(1)} %get-tuple-element.2) | data formatting | bytes 393216
  47.2 0.6 %copy.9 = f32[3,4,8,256]{3,2,1,0:T(8,128)} copy(f32[3,4,8,256]{3,2,1,0:T(8,128)S(1)} %get-tuple-element.3) | data formatting | bytes 196608

commit v5 on v4

--- a/solution.py
+++ b/solution.py
@@ -360,6 +360,14 @@
         copy.wait_send()
 
 
+def store_both(first, second, first_out, second_out, done):
+    copies = [pltpu.make_async_copy(first, first_out, done.at[0]), pltpu.make_async_copy(second, second_out, done.at[1])]
+    for copy in copies:
+        copy.start()
+    for copy in copies:
+        copy.wait()
+
+
 def on_device(velocity, strain, row_bins, cotangent):
     def buf(*shape):
         return pltpu.VMEM(shape, jnp.float32)
@@ -378,7 +386,7 @@
         pltpu.SemaphoreType.DMA((64,)), pltpu.SemaphoreType.DMA((64,)), pltpu.SemaphoreType.DMA((4,)),
         pltpu.SemaphoreType.REGULAR,
     ]
-    return pl.pallas_call(
+    results = pl.pallas_call(
         kernel,
         out_shape=(
             pltpu.VMEM(strain.shape, jnp.float32),
@@ -391,6 +399,13 @@
             collective_id=1, has_side_effects=True, vmem_limit_bytes=32 * 1024 * 1024),
         cost_estimate=pl.CostEstimate(flops=3_000_000, bytes_accessed=800_000, transcendentals=8192),
     )(*[pltpu.with_memory_space_constraint(v, pltpu.HBM) for v in (velocity, strain, row_bins, cotangent)])
+    return pl.pallas_call(
+        store_both,
+        out_shape=(pltpu.HBM(strain.shape, jnp.float32), pltpu.HBM(velocity.shape, jnp.float32)),
+        in_specs=[vmem, vmem],
+        out_specs=(hbm, hbm),
+        scratch_shapes=[pltpu.SemaphoreType.DMA((2,))],
+    )(*[pltpu.with_memory_space_constraint(v, pltpu.VMEM) for v in results])
 
 
 def solution(mesh):

time: 48 us -> 47.4 us (0.987)
  local copies, waits for them, and re-layouts: 1.32 us -> 0 us
  Pallas kernels: 45.9 us -> 46.6 us
    unnamed x2 -> x0, local copies, waits for them, and re-layouts: 1.32 us -> none
    pallas_call x0 -> x1, Pallas kernels: none -> 0.72 us  [on_device(): pl.pallas_call(store_both, out_shape=(pltpu.HBM(strain.shape, jnp.float32...]
where the time goes in v5:
time: 47.4 us; the launch traced here: 47.3 us
  Pallas kernels  46.6 us (98%)
  between operations  0.64 us (1%)
    pallas_call x1, Pallas kernels, on_device(): pl.pallas_call(kernel, out_shape=(pltpu.VMEM(strain.shape, jnp.float32),...  45.9 us

profile of v5, /device:TPU:8, one launch (start us, length us, event | category | flops | bytes accessed | tf_op | source)
XLA Modules:
  0.0 47.3 jit_solution(12989665484014547602)
XLA Ops:
  0.6 45.9 %shard_map.59 = (f32[6,4,8,256]{3,2,1,0:T(8,128)S(1)}, f32[3,4,8,256]{3,2,1,0:T(8,128)S(1)}) custom-call(f32[3,4,8,256]{3,2,1,0:T(8,128)} %vel_in.1, f32[6,4,8,256]{3,2,1,0:T(8,128)} %strain_in.1, s32[8]{0:T(128)} %bins_in.1, f32[6,4,8,256]{3,2,1,0:T(8,128)} %cot_in.1), custom_call_target="tpu_custom_call" | custom-call | flops 3000000 | bytes 800000 | tf_op jit(solution)/shard_map/pallas_call | solution.py:389
  46.6 0.7 %shard_map.60 = (f32[6,4,8,256]{3,2,1,0:T(8,128)}, f32[3,4,8,256]{3,2,1,0:T(8,128)}) custom-call(f32[6,4,8,256]{3,2,1,0:T(8,128)S(1)} %get-tuple-element.4.first, f32[3,4,8,256]{3,2,1,0:T(8,128)S(1)} %get-tuple-element.5.second), custom_call_target="tpu_custom_call" | custom-call | tf_op jit(solution)/shard_map/pallas_call | solution.py:402

commit v6 on v5

--- a/solution.py
+++ b/solution.py
@@ -57,7 +57,7 @@
            e1, rb1, pa1, zb1, g1, ag1,
            ec, rbc, pac, zbc,
            e2, rb2, pa2, zb2, g2, ag2,
-           t1, ts, t3, tz,
+           t0, ts, t1, tz,
            send, recv, load, gate):
     span, stream = lax.axis_index("span"), lax.axis_index("stream")
     h, y = span // RING, lax.rem(span, RING)
@@ -165,12 +165,11 @@
         own_bins = jnp.where(row == i, value, own_bins)
         lane_bins = jnp.where(column == i, value, lane_bins)
 
+    t0[...] = lane_bins[0:1]
+
     def packed(three):
         wide = jnp.where(kind == 0, three[0], jnp.where(kind == 1, three[1], jnp.where(kind == 2, three[2], 0.0)))
         return jnp.sum(jnp.where(column == row, wide, 0.0), axis=0, keepdims=True)
-
-    def columns_of(wide, mask):
-        return [jnp.sum(jnp.where(mask & (kind == q), wide, 0.0), axis=-1, keepdims=True) for q in range(3)]
 
     @pl.when(core == 1)
     def _():
@@ -201,6 +200,7 @@
     for k in range(6):
         keep_ends(ec, k, [cot[k, i] for i in range(CELLS)])
     first_cot = scatter(ec, rbc, slice(0, 6))
+    near_bins = [push(t0, ts.at[n], stream_id(s)) for n, s in enumerate(STREAM_STEPS)]
     for at, copy in zip((early, late), crossed):
         arrive([copy])
         entering = CLOSE * (zb1[at] + AROUND * pa1[at])
@@ -270,9 +270,14 @@
     def over_lanes(values):
         return jnp.sum(values[:, :128] + values[:, 128:], axis=-1, keepdims=True)
 
-    t1[0:1] = packed([over_lanes(cross), over_lanes(square), over_lanes(blame)])
-    t1[1:2] = lane_bins[0:1]
-    near = [push(t1, ts.at[n], stream_id(s)) for n, s in enumerate(STREAM_STEPS)]
+    t1[...] = packed([over_lanes(cross), over_lanes(square), over_lanes(blame)])
+    everywhere = []
+    for far, turn in ((1, 0), (1, 1), (1, 3), (1, 2), (0, 2), (0, 1), (0, 3), (0, 0)):
+        there = (h + far - 2 * h * far) * RING + ring_peer(turn)
+        for n, step in enumerate(STREAM_STEPS + (0,)):
+            if (far, turn, step) != (0, 0, 0):
+                everywhere.append(push(t1, tz.at[n, 4 * far + turn], (there, lax.rem(stream + step + 64, 64))))
+    tz[4, 0] = t1[...]
     for a in range(3):
         with_filtered(a, 2, lambda k, i: WEIGHTS[k] * leo[k, i])
     second.append(scatter(e2, rb2, parts[2]))
@@ -286,19 +291,17 @@
         over2.append(push(pa2.at[at], zb2.at[at], across))
 
     cross_part(0)
-    arrive(near)
-    wide = jnp.where(own_bins == t1[1:2], t1[0:1], 0.0)
-    for n in range(4):
-        wide = wide + jnp.where(own_bins == ts[n, 1:2], ts[n, 0:1], 0.0)
-    t3[...] = packed(columns_of(wide, True))
-    everywhere = [push(t3, tz.at[d - 1], (lax.rem(span + d, 8), stream)) for d in (4, 3, 5, 2, 6, 1, 7)]
     cross_part(1)
     cross_part(2)
+    arrive(near_bins)
     arrive(everywhere)
-    total = t3[...]
-    for d in range(7):
-        total = total + tz[d]
-    sums = columns_of(jnp.broadcast_to(total, (8, 128)), column == row)
+    wide = jnp.zeros((8, 128), jnp.float32)
+    for n in range(5):
+        total = tz[n, 0]
+        for slot in range(1, 8):
+            total = total + tz[n, slot]
+        wide = wide + jnp.where(own_bins == (ts[n] if n < 4 else t0[...]), total, 0.0)
+    sums = [jnp.sum(jnp.where(kind == q, wide, 0.0), axis=-1, keepdims=True) for q in range(3)]
     denominator = jnp.broadcast_to(sums[1], (8, 128)) + EPSILON
     coefficient = jnp.broadcast_to(sums[0], (8, 128)) / denominator
     row_cross = -jnp.broadcast_to(sums[2], (8, 128)) / denominator
@@ -339,6 +342,8 @@
             weighted = WEIGHTS[k] * row_cross
             leo[k, i] = bar + weighted * model
             mod[k, i] = weighted * leonard - coefficient * bar + (WEIGHTS[k] * row_square) * model
+    for copy in copies[:-6]:
+        copy.wait_send()
     arrive(last)
     for half in (0, 1):
         lanes = slice(128 * half, 128 * half + 128)
@@ -356,7 +361,7 @@
         for a in range(3):
             for i in range(CELLS):
                 grad[a, i, :, lanes] = sums[a][i]
-    for copy in copies:
+    for copy in copies[-6:]:
         copy.wait_send()
 
 
@@ -382,8 +387,8 @@
         buf(4, 6, 8, 128), buf(4, 6, 8, 128), buf(6, 8, 128), buf(6, 8, 128),
         buf(4, 15, 8, 128), buf(4, 15, 8, 128), buf(15, 8, 128), buf(15, 8, 128), buf(4, 9, 8, 128),
         buf(4, 9, 8, 128),
-        buf(2, 128), buf(4, 2, 128), buf(1, 128), buf(7, 1, 128),
-        pltpu.SemaphoreType.DMA((64,)), pltpu.SemaphoreType.DMA((64,)), pltpu.SemaphoreType.DMA((4,)),
+        buf(1, 128), buf(4, 1, 128), buf(1, 128), buf(5, 8, 1, 128),
+        pltpu.SemaphoreType.DMA((96,)), pltpu.SemaphoreType.DMA((96,)), pltpu.SemaphoreType.DMA((4,)),
         pltpu.SemaphoreType.REGULAR,
     ]
     results = pl.pallas_call(

time: 47.4 us -> 46.1 us (0.973)
  the two profiles are of different devices: /device:TPU:8 before, /device:TPU:38 now
where the time goes in v6:
time: 46.1 us; the launch traced here: 46 us
  Pallas kernels  45.4 us (98%)
  between operations  0.64 us (1%)
    pallas_call x1, Pallas kernels, on_device(): pl.pallas_call(kernel, out_shape=(pltpu.VMEM(strain.shape, jnp.float32),...  44.6 us

profile of v6, /device:TPU:38, one launch (start us, length us, event | category | flops | bytes accessed | tf_op | source)
XLA Modules:
  0.0 46.0 jit_solution(16828551735999047116)
XLA Ops:
  0.6 44.6 %shard_map.59 = (f32[6,4,8,256]{3,2,1,0:T(8,128)S(1)}, f32[3,4,8,256]{3,2,1,0:T(8,128)S(1)}) custom-call(f32[3,4,8,256]{3,2,1,0:T(8,128)} %vel_in.1, f32[6,4,8,256]{3,2,1,0:T(8,128)} %strain_in.1, s32[8]{0:T(128)} %bins_in.1, f32[6,4,8,256]{3,2,1,0:T(8,128)} %cot_in.1), custom_call_target="tpu_custom_call" | custom-call | flops 3000000 | bytes 800000 | tf_op jit(solution)/shard_map/pallas_call | solution.py:394
  45.3 0.7 %shard_map.60 = (f32[6,4,8,256]{3,2,1,0:T(8,128)}, f32[3,4,8,256]{3,2,1,0:T(8,128)}) custom-call(f32[6,4,8,256]{3,2,1,0:T(8,128)S(1)} %get-tuple-element.4.first, f32[3,4,8,256]{3,2,1,0:T(8,128)S(1)} %get-tuple-element.5.second), custom_call_target="tpu_custom_call" | custom-call | tf_op jit(solution)/shard_map/pallas_call | solution.py:407

commit v7 on v6

--- a/solution.py
+++ b/solution.py
@@ -142,8 +142,8 @@
         ((vel_in, vel), (strain_in, strain), (cot_in, cot), (bins_in, bins)))]
     for one in loads:
         one.start()
-    for one in loads:
-        one.wait()
+    loads[0].wait()
+    loads[1].wait()
 
     for a in range(3):
         fields[a] = vel[a]
@@ -154,6 +154,19 @@
     fields[3] = jnp.sqrt(jnp.maximum(2.0 * total, STRAIN_FLOOR))
     for f in range(10):
         keep_ends(e1, f, [fields[f, i] for i in range(CELLS)])
+    @pl.when(core == 1)
+    def _():
+        pl.semaphore_wait(barrier, 2 * (RING - 1) + 1)
+        greet(gate, (span, stream - 1))
+
+    @pl.when(core == 0)
+    def _():
+        pl.semaphore_wait(gate, 1)
+
+    early, late = slice(0, 4), slice(4, 10)
+    scattered = [scatter(e1, rb1, at) for at in (early, late)]
+    loads[2].wait()
+    loads[3].wait()
     row = lax.broadcasted_iota(jnp.int32, (8, 128), 0)
     lane = lax.broadcasted_iota(jnp.int32, (8, 128), 1)
     column = lax.rem(lane, 8)
@@ -171,17 +184,6 @@
         wide = jnp.where(kind == 0, three[0], jnp.where(kind == 1, three[1], jnp.where(kind == 2, three[2], 0.0)))
         return jnp.sum(jnp.where(column == row, wide, 0.0), axis=0, keepdims=True)
 
-    @pl.when(core == 1)
-    def _():
-        pl.semaphore_wait(barrier, 2 * (RING - 1) + 1)
-        greet(gate, (span, stream - 1))
-
-    @pl.when(core == 0)
-    def _():
-        pl.semaphore_wait(gate, 1)
-
-    early, late = slice(0, 4), slice(4, 10)
-    scattered = [scatter(e1, rb1, at) for at in (early, late)]
     crossed, arrived = [], []
     for at, group in zip((early, late), scattered):
         arrive(group)
@@ -209,6 +211,10 @@
             entering = rb1[p, at] + STEP * entering
             g1[p + 1, at] = entering
         arrived.append(spread(g1, ag1, at))
+        if len(arrived) == 1:
+            arrive(first_cot)
+            pac[...] = carry([rbc[p] for p in range(RING)])
+            over_cot = push(pac, zbc, across)
     arrive(arrived[0])
     for f in range(4):
         for half in (0, 1):
@@ -250,10 +256,6 @@
         with_filtered(a, 1, lambda k, i: WEIGHTS[k] * mod[k, i])
     second.append(scatter(e2, rb2, parts[1]))
 
-    arrive(first_cot)
-    pac[...] = carry([rbc[p] for p in range(RING)])
-    over_cot = push(pac, zbc, across)
-
     arrive(arrived[1])
     cross = jnp.zeros((8, 256), jnp.float32)
     for k, (a, b) in enumerate(PAIRS):
@@ -272,11 +274,16 @@
 
     t1[...] = packed([over_lanes(cross), over_lanes(square), over_lanes(blame)])
     everywhere = []
-    for far, turn in ((1, 0), (1, 1), (1, 3), (1, 2), (0, 2), (0, 1), (0, 3), (0, 0)):
-        there = (h + far - 2 * h * far) * RING + ring_peer(turn)
-        for n, step in enumerate(STREAM_STEPS + (0,)):
-            if (far, turn, step) != (0, 0, 0):
-                everywhere.append(push(t1, tz.at[n, 4 * far + turn], (there, lax.rem(stream + step + 64, 64))))
+
+    def tell(far, turns):
+        there = h + far - 2 * h * far
+        for turn in turns:
+            for n, step in enumerate(STREAM_STEPS + (0,)):
+                if (far, turn, step) != (0, 0, 0):
+                    everywhere.append(push(t1, tz.at[n, 4 * far + turn],
+                                           (there * RING + ring_peer(turn), lax.rem(stream + step + 64, 64))))
+
+    tell(1, (2, 1, 3, 0))
     tz[4, 0] = t1[...]
     for a in range(3):
         with_filtered(a, 2, lambda k, i: WEIGHTS[k] * leo[k, i])
@@ -290,6 +297,7 @@
         pa2[at] = carry([rb2[p, at] for p in range(RING)])
         over2.append(push(pa2.at[at], zb2.at[at], across))
 
+    tell(0, (2, 1, 3, 0))
     cross_part(0)
     cross_part(1)
     cross_part(2)

time: 46.1 us -> 45.8 us (level)
  no operation moved by 1% of the time
where the time goes in v7:
time: 45.8 us; the launch traced here: 45.7 us
  Pallas kernels  45 us (98%)
  between operations  0.64 us (1%)
    pallas_call x1, Pallas kernels, on_device(): pl.pallas_call(kernel, out_shape=(pltpu.VMEM(strain.shape, jnp.float32),...  44.3 us

profile of v7, /device:TPU:38, one launch (start us, length us, event | category | flops | bytes accessed | tf_op | source)
XLA Modules:
  0.0 45.7 jit_solution(4530729754034691957)
XLA Ops:
  0.6 44.3 %shard_map.59 = (f32[6,4,8,256]{3,2,1,0:T(8,128)S(1)}, f32[3,4,8,256]{3,2,1,0:T(8,128)S(1)}) custom-call(f32[3,4,8,256]{3,2,1,0:T(8,128)} %vel_in.1, f32[6,4,8,256]{3,2,1,0:T(8,128)} %strain_in.1, s32[8]{0:T(128)} %bins_in.1, f32[6,4,8,256]{3,2,1,0:T(8,128)} %cot_in.1), custom_call_target="tpu_custom_call" | custom-call | flops 3000000 | bytes 800000 | tf_op jit(solution)/shard_map/pallas_call | solution.py:402
  45.0 0.7 %shard_map.60 = (f32[6,4,8,256]{3,2,1,0:T(8,128)}, f32[3,4,8,256]{3,2,1,0:T(8,128)}) custom-call(f32[6,4,8,256]{3,2,1,0:T(8,128)S(1)} %get-tuple-element.4.first, f32[3,4,8,256]{3,2,1,0:T(8,128)S(1)} %get-tuple-element.5.second), custom_call_target="tpu_custom_call" | custom-call | tf_op jit(solution)/shard_map/pallas_call | solution.py:415

commit v8 on v7

--- a/solution.py
+++ b/solution.py
@@ -125,18 +125,18 @@
 
     def chip_id(step):
         there, position = stream_id(2 * step)
-        return (there, position - core)
+        return (there, position - core + 1)
 
     barrier = pltpu.get_barrier_semaphore()
-    greet(barrier, (across[0], this_chip))
+    greet(barrier, (across[0], this_chip + 1))
     for d in (2, 1, 3):
-        greet(barrier, (h * RING + ring_peer(d), this_chip + 1))
+        greet(barrier, (h * RING + ring_peer(d), this_chip))
     greet(barrier, chip_id(-1))
     greet(barrier, chip_id(1))
 
-    @pl.when(core == 0)
+    @pl.when(core == 1)
     def _():
-        greet(barrier, (span, stream + 1))
+        greet(barrier, (span, stream - 1))
 
     loads = [pltpu.make_async_copy(src, dst, load.at[n]) for n, (src, dst) in enumerate(
         ((vel_in, vel), (strain_in, strain), (cot_in, cot), (bins_in, bins)))]
@@ -154,12 +154,12 @@
     fields[3] = jnp.sqrt(jnp.maximum(2.0 * total, STRAIN_FLOOR))
     for f in range(10):
         keep_ends(e1, f, [fields[f, i] for i in range(CELLS)])
-    @pl.when(core == 1)
+    @pl.when(core == 0)
     def _():
         pl.semaphore_wait(barrier, 2 * (RING - 1) + 1)
-        greet(gate, (span, stream - 1))
-
-    @pl.when(core == 0)
+        greet(gate, (span, stream + 1))
+
+    @pl.when(core == 1)
     def _():
         pl.semaphore_wait(gate, 1)
 
@@ -189,12 +189,12 @@
         arrive(group)
         pa1[at] = carry([rb1[p, at] for p in range(RING)])
         if not crossed:
-            @pl.when(core == 0)
+            @pl.when(core == 1)
             def _():
                 pl.semaphore_wait(barrier, 2 + 2 * 2)
-                greet(gate, (span, stream + 1))
-
-            @pl.when(core == 1)
+                greet(gate, (span, stream - 1))
+
+            @pl.when(core == 0)
             def _():
                 pl.semaphore_wait(gate, 1)
 
@@ -235,8 +235,8 @@
             square = square + weighted[i] * model
             blame = blame + cot[k, i] * model
         keep_ends(e2, k, weighted)
-    parts = (slice(0, 6), slice(6, 12), slice(12, 15))
-    second = [scatter(e2, rb2, parts[0])]
+    parts = (slice(0, 3), slice(3, 6), slice(6, 12), slice(12, 15))
+    second = [scatter(e2, rb2, parts[0]), scatter(e2, rb2, parts[1])]
 
     def with_filtered(a, slot, field):
         cells = []
@@ -254,7 +254,7 @@
     for a in range(3):
         with_filtered(a, 0, lambda k, i: cot[k, i])
         with_filtered(a, 1, lambda k, i: WEIGHTS[k] * mod[k, i])
-    second.append(scatter(e2, rb2, parts[1]))
+    second.append(scatter(e2, rb2, parts[2]))
 
     arrive(arrived[1])
     cross = jnp.zeros((8, 256), jnp.float32)
@@ -287,7 +287,7 @@
     tz[4, 0] = t1[...]
     for a in range(3):
         with_filtered(a, 2, lambda k, i: WEIGHTS[k] * leo[k, i])
-    second.append(scatter(e2, rb2, parts[2]))
+    second.append(scatter(e2, rb2, parts[3]))
 
     over2 = []
 
@@ -301,6 +301,7 @@
     cross_part(0)
     cross_part(1)
     cross_part(2)
+    cross_part(3)
     arrive(near_bins)
     arrive(everywhere)
     wide = jnp.zeros((8, 128), jnp.float32)
@@ -329,10 +330,10 @@
         return (spare * buf[(*p, slice(6, 9))] - row_model * buf[(*p, slice(9, 12))]
                 - row_cross * buf[(*p, slice(12, 15))])
 
-    arrive([over_cot, over2[0]])
+    arrive([over_cot] + over2[:2])
     last = adjoint(slice(3, 9), [rbc[p] + row_cross * rb2[p, 0:6] for p in range(RING)],
                    zbc[...] + row_cross * zb2[0:6])
-    arrive(over2[1:])
+    arrive(over2[2:])
     last = last + adjoint(slice(0, 3), [coarse_part(rb2, p) for p in range(RING)], coarse_part(zb2))
 
     def wide(values):

time: 45.8 us -> 45.4 us (level)
  the two profiles are of different devices: /device:TPU:38 before, /device:TPU:10 now
where the time goes in v8:
time: 45.4 us; the launch traced here: 45.3 us
  Pallas kernels  44.7 us (98%)
  between operations  0.64 us (1%)
    pallas_call x1, Pallas kernels, on_device(): pl.pallas_call(kernel, out_shape=(pltpu.VMEM(strain.shape, jnp.float32),...  43.9 us

profile of v8, /device:TPU:10, one launch (start us, length us, event | category | flops | bytes accessed | tf_op | source)
XLA Modules:
  0.0 45.3 jit_solution(5300062287043573910)
XLA Ops:
  0.6 43.9 %shard_map.59 = (f32[6,4,8,256]{3,2,1,0:T(8,128)S(1)}, f32[3,4,8,256]{3,2,1,0:T(8,128)S(1)}) custom-call(f32[3,4,8,256]{3,2,1,0:T(8,128)} %vel_in.1, f32[6,4,8,256]{3,2,1,0:T(8,128)} %strain_in.1, s32[8]{0:T(128)} %bins_in.1, f32[6,4,8,256]{3,2,1,0:T(8,128)} %cot_in.1), custom_call_target="tpu_custom_call" | custom-call | flops 3000000 | bytes 800000 | tf_op jit(solution)/shard_map/pallas_call | solution.py:403
  44.6 0.7 %shard_map.60 = (f32[6,4,8,256]{3,2,1,0:T(8,128)}, f32[3,4,8,256]{3,2,1,0:T(8,128)}) custom-call(f32[6,4,8,256]{3,2,1,0:T(8,128)S(1)} %get-tuple-element.4.first, f32[3,4,8,256]{3,2,1,0:T(8,128)S(1)} %get-tuple-element.5.second), custom_call_target="tpu_custom_call" | custom-call | tf_op jit(solution)/shard_map/pallas_call | solution.py:416
